TPU v7x, 512 devices: a whole 4x8x8 slice. The times are simulated.
512 devices in a mesh: row: 32 (over z_lo, x, core), col: 16 (over z_hi, y).
Axes of the slice: x: 4, y: 8, z: 8 (z_hi: 2, z_lo: 4; z = z_hi * 4 + z_lo), core: 2. Of those that a mesh axis runs over, the one named last changes fastest.
Arguments:
- pair: bfloat16 [768, 768, 128], P('row', 'col'), may hold values from -6 to 6
- valid: int32 [768], replicated, may hold values 0 or 1
- ln_gain: float32 [128], replicated, may hold values from 0.1 to 1.9
- w_query: bfloat16 [128, 128], replicated, may hold values from -3 to 3
- w_key: bfloat16 [128, 128], replicated, may hold values from -3 to 3
- w_value: bfloat16 [128, 128], replicated, may hold values from -0.5 to 0.5
- w_gate: bfloat16 [128, 128], replicated, may hold values from -0.5 to 0.5
- w_bias: bfloat16 [128, 4], replicated, may hold values from -0.5 to 0.5
- w_out: bfloat16 [128, 128], replicated, may hold values from -0.5 to 0.5
Outputs:
- update: bfloat16 [768, 768, 128], P('row', 'col')
All inputs are finite; a program needn't handle non-finite values.
Results may differ from a plain program's by a relative error of at most 0.015.
The roundings to bfloat16 on the way count: a program that leaves them out, or rounds other values in their place, can miss the bound.
Values may be sent and summed in bfloat16 or wider, within the bound.
No kernel may reach another device: no remote copies, remote signals or barrier semaphores. Data moves between devices by JAX's collectives and lax.ppermute only.
A program may use at most 64 MiB of HBM per device.

v0:
```python
import jax
import jax.numpy as jnp
from jax import lax
from jax.sharding import PartitionSpec as P


def from_root(value, axis, source):
    kept = jnp.where(lax.axis_index(axis) == source, value, 0).astype(value.dtype)
    return lax.psum(kept, axis)


def normalize(pair, ln_gain):
    values = pair.astype(jnp.float32)
    center = jnp.mean(values, axis=-1, keepdims=True)
    spread = jnp.mean((values - center) ** 2, axis=-1, keepdims=True)
    return ((values - center) * lax.rsqrt(spread + 1e-05) * ln_gain).astype(jnp.bfloat16)


def local(pair, valid, ln_gain, w_query, w_key, w_value, w_gate, w_bias, w_out):
    width = pair.shape[2]
    heads = w_bias.shape[1]
    joined = w_query.shape[1]
    head_size = joined // heads
    normed = normalize(pair, ln_gain)
    local_bias = jnp.einsum(
        "ijc,ch->hij", normed, w_bias, preferred_element_type=jnp.float32
    ).astype(jnp.bfloat16)
    bias_full_rows = lax.all_gather(local_bias, "col", axis=2, tiled=True)
    group = 1
    rows_here, cols_here = (normed.shape[0], normed.shape[1])
    flat = normed.reshape(rows_here * cols_here, width)
    query = (
        jnp.dot(flat, w_query, preferred_element_type=jnp.float32) * head_size ** (-0.5)
    ).astype(jnp.bfloat16)
    query = query.reshape(rows_here, cols_here, heads, head_size)
    gate = jax.nn.sigmoid(jnp.dot(flat, w_gate, preferred_element_type=jnp.float32))
    blocks_per = group * lax.axis_size("row") // lax.axis_size("col")
    received = []
    for offset in range(blocks_per):
        received.append(
            from_root(bias_full_rows, "row", blocks_per * (lax.axis_index("col") // group) + offset)
        )
    bias_block = jnp.concatenate(received, axis=1)
    penalty = jnp.where(valid == 1, 0.0, -1000000000.0).astype(jnp.float32)
    w_both = jnp.concatenate([w_key, w_value], axis=1)
    start_peak = jnp.full((heads, rows_here, cols_here), -1e30, jnp.float32)
    piece = lax.all_gather(normed, "col", axis=1, tiled=True)
    count = piece.shape[1]
    projected = jnp.einsum("ikc,ce->ike", piece, w_both, preferred_element_type=jnp.float32).astype(
        jnp.bfloat16
    )
    keys = projected[:, :, :joined].reshape(rows_here, count, heads, head_size)
    values = projected[:, :, joined:].reshape(rows_here, count, heads, head_size)
    scores = jnp.einsum("ijhd,ikhd->hijk", query, keys, preferred_element_type=jnp.float32)
    bias_piece = bias_block.astype(jnp.float32)
    scores = scores + bias_piece[:, None, :, :] + penalty
    new_peak = jnp.maximum(start_peak, jnp.max(scores, axis=-1))
    weights = jnp.exp(scores - new_peak[..., None])
    total = jnp.sum(weights, axis=-1)
    contrib = jnp.einsum(
        "hijk,ikhd->ijhd", weights.astype(jnp.bfloat16), values, preferred_element_type=jnp.float32
    )
    result = (new_peak, total, contrib)
    final_peak, final_total, final_numer = result
    attended = final_numer / jnp.transpose(final_total, (1, 2, 0))[..., None]
    gated = (attended.reshape(rows_here * cols_here, joined) * gate).astype(jnp.bfloat16)
    update = jnp.dot(gated, w_out, preferred_element_type=jnp.float32).astype(jnp.bfloat16)
    update = update.reshape(rows_here, cols_here, width)
    return update


def solution(mesh):
    return jax.shard_map(
        local,
        mesh=mesh,
        in_specs=(P("row", "col", None), P(), P(), P(), P(), P(), P(), P(), P()),
        out_specs=P("row", "col", None),
        check_vma=False,
    )
```

profile of v0, /device:TPU:1, one launch (start us, length us, event | category | flops | bytes accessed | tf_op | source)
XLA Modules:
  0.0 450.2 jit_solution(3367165472909107480)
XLA Ops:
  7.4 0.0 copy-start
  7.4 0.0 all-reduce.3.cloned.1.call-start
  7.4 1.2 convert_reduce_fusion
  8.6 1.4 fusion.19
  10.0 1.3 fusion.21
  11.4 0.0 copy-start.2
  11.4 1.1 fusion.16
  12.5 0.1 copy.40
  12.6 57.6 %all_gather.7 = bf16[4,24,768]{1,0,2:T(4,128)(2,1)S(1)} all-gather(bf16[4,24,48]{1,0,2:T(4,128)(2,1)S(1)} %copy.40), channel_id=1, replica_groups=mesh['row'=32,'col'=16] {'col'}, dimensions={2}, use_global_device_ids=true | all-gather | bytes 156672 | tf_op jit(solution)/shard_map/all_gather | solution.py:28
  70.2 1.7 broadcast_select_fusion.1
  72.0 0.0 all-reduce.3.cloned.1.call-update
  72.0 0.0 all-gather.2.cloned.1.call-start
  72.1 0.0 copy-done.2
  72.1 0.5 all-gather.2.cloned.1.call-update
  72.6 0.0 copy-done.4
  72.6 0.1 copy.35
  72.7 0.1 copy.36
  72.8 0.0 copy-done
  72.8 1.2 fusion.12
  74.0 1.5 reshape.59
  75.5 335.6 %all-reduce.3.cloned.1.call-done = (bf16[4,24,768]{1,0,2:T(4,128)(2,1)}, bf16[4,24,768]{1,0,2:T(4,128)(2,1)}) async-done(((bf16[4,24,768]{1,0,2:T(4,128)(2,1)}, bf16[4,24,768]{1,0,2:T(4,128)(2,1)}), (bf16[4,24,768]{1,0,2:T(4,128)(2,1)}, bf16[4,24,768]{1,0,2:T(4,128)(2,1)})) %all-reduce.3.cloned.1.call-update) | async-done | bytes 294928 | tf_op jit(solution)/shard_map/psum | solution.py:9
  411.2 1.4 copy.42
  412.6 1.4 copy.41
  414.0 0.9 maximum_convert_fusion
  414.9 5.0 %convolution_convert_fusion = bf16[24,768,256]{1,2,0:T(8,128)(2,1)S(1)} fusion(bf16[24,768,128]{2,1,0:T(8,128)(2,1)} %all-gather.2.cloned.1.call-done, bf16[128,128]{0,1:T(8,128)(2,1)S(1)} %copy.36, bf16[128,128]{0,1:T(8,128)(2,1)S(1)} %copy.35), kind=kOutput, calls=%fused_computation.7 | convolution fusion | flops 1212809216 | bytes 14221312 | tf_op jit(solution)/shard_map/ikc,ce->ike/dot_general | solution.py:49
  419.9 4.2 fusion.28
  424.0 5.1 %fusion = (f32[4,24,48]{2,1,0:T(8,128)S(1)}, f32[4,24,48,768]{3,2,1,0:T(8,128)S(1)}) fusion(f32[768]{0:T(1024)S(1)} %compare_select_fusion, f32[4,48,768]{2,1,0:T(8,128)} %maximum_convert_fusion, bf16[24,768,4,32]{1,3,2,0:T(8,128)(2,1)} %bitcast.23, bf16[24,48,4,32]{3,2,1,0:T(4,128)(2,1)} %reshape.59), kind=kOutput, calls=%fused_computation.2 | convolution fusion | flops 237104640 | bytes 19780608 | tf_op jit(solution)/shard_map/ijhd,ikhd->hijk/dot_general | solution.py:54
  429.1 3.9 fusion.1
  433.0 5.5 %bitcast_divide_fusion = f32[24,48,4,32]{1,3,2,0:T(8,128)} fusion(bf16[24,768,4,32]{1,3,2,0:T(8,128)(2,1)} %bitcast.26, bf16[4,24,48,768]{3,2,1,0:T(8,128)(2,1)S(1)} %get-tuple-element.8, f32[24,48,4]{1,2,0:T(4,128)S(1)} %copy.44), kind=kOutput, calls=%fused_computation.19 | convolution fusion | flops 226639872 | bytes 12404736 | tf_op jit(solution)/shard_map/hijk,ikhd->ijhd/dot_general | solution.py:60
  438.5 2.1 copy.49
  440.6 1.0 reshape.60
  441.6 1.1 convolution_convert_fusion.1
  (19 shorter events, 0.1 us)
Async XLA Ops:
  7.4 65.5 %copy-start = (bf16[128,128]{1,0:T(8,128)(2,1)S(1)}, bf16[128,128]{1,0:T(8,128)(2,1)}, u32[]{:S(2)}) copy-start(bf16[128,128]{1,0:T(8,128)(2,1)} %param.12) | copy-start | bytes 98308
  7.4 65.2 %copy-start.4 = (bf16[128,128]{1,0:T(8,128)(2,1)S(1)}, bf16[128,128]{1,0:T(8,128)(2,1)}, u32[]{:S(2)}) copy-start(bf16[128,128]{1,0:T(8,128)(2,1)} %param.13) | copy-start | bytes 98308
  7.4 65.3 %copy-start.5 = (bf16[128,128]{1,0:T(8,128)(2,1)S(1)}, bf16[128,128]{1,0:T(8,128)(2,1)}, u32[]{:S(2)}) copy-start(bf16[128,128]{1,0:T(8,128)(2,1)} %param.14) | copy-start | bytes 98308
  7.4 68.2 %copy-start.6 = (s32[768]{0:T(1024)S(1)}, s32[768]{0:T(1024)}, u32[]{:S(2)}) copy-start(s32[768]{0:T(1024)} %param.10) | copy-start | bytes 9220
  7.4 403.8 %all-reduce.3.cloned.1.call-start = ((), (), s32[]{:S(2)}) async-start(), calls=%async_computation.1 | async-start | bytes 3145728 | tf_op jit(solution)/shard_map/psum | solution.py:9
  11.4 60.7 %copy-start.2 = (bf16[24,48,128]{2,1,0:T(8,128)(2,1)}, bf16[24,48,128]{2,1,0:T(8,128)(2,1)S(1)}, u32[]{:S(2)}) copy-start(bf16[24,48,128]{2,1,0:T(8,128)(2,1)S(1)} %fusion.21) | copy-start | bytes 884740
  72.0 342.9 %all-gather.2.cloned.1.call-start = ((), (), s32[]{:S(2)}) async-start(), calls=%async_computation | async-start | bytes 5013504 | tf_op jit(solution)/shard_map/all_gather | solution.py:47
  424.0 5.1 %copy-start.1 = (f32[4,48,768]{2,1,0:T(8,128)S(1)}, f32[4,48,768]{2,1,0:T(8,128)}, u32[]{:S(2)}) copy-start(f32[4,48,768]{2,1,0:T(8,128)} %maximum_convert_fusion) | copy-start | bytes 1769476
  438.5 3.1 copy-start.3
  438.5 3.1 copy-start.7
  438.5 3.1 copy-start.8
Sparse Core Ops, SparseCore 0:
  72.1 338.9 all-reduce.2
Sparse Core Ops, SparseCore 1:
  75.7 136.1 all-gather.1
where the time goes:
time: 451 us; the launch traced here: 450 us
  waiting for transfers between devices  336 us (75%)
  blocking collectives  57.6 us (13%)
  matrix products  18.9 us (4%)
  between operations  15.1 us (3%)
  local copies, waits for them, and re-layouts  12 us (3%)
  other arithmetic  10.4 us (2%)
    psum x1, waiting for transfers between devices, from_root(): return lax.psum(kept, axis)  336 us
    all_gather x1, blocking collectives, local(): bias_full_rows = lax.all_gather(local_bias, 'col', axis=2, tiled=True)  57.6 us
  transfers between devices with their start and end apart: 2, of which 1 were waited for; matrix products, arithmetic and copies ran while one was open for 1% of the time, Pallas kernels for 0%

commit v1 on v0

v1 whole, which is shorter than its diff:
```python
import jax
import jax.numpy as jnp
from jax import lax
from jax.experimental import pallas as pl
from jax.experimental.pallas import tpu as pltpu
from jax.sharding import Mesh
from jax.sharding import PartitionSpec as P

HEADS = 4
HEAD_DIM = 32
ROW = ("zl", "x", "core")
COL = ("zh", "yo", "yi")
NT = (((1,), (1,)), ((), ()))


def head_mask(rows, h):
    lane = lax.broadcasted_iota(jnp.int32, (rows, 128), 1)
    return lane // HEAD_DIM == h


def normalize_kernel(pair_ref, gain_ref, w_ref, normed_ref, bias_ref):
    rows, cols, width = pair_ref.shape
    line = lax.broadcasted_iota(jnp.int32, (128, width), 0)
    w_t = w_ref[...].astype(jnp.float32)
    wide = sum(jnp.where(line // rows == h, w_t[h : h + 1, :], 0.0) for h in range(HEADS))
    acc = jnp.zeros((cols, 128), jnp.float32)
    for j in range(rows):
        values = pair_ref[j].astype(jnp.float32)
        center = jnp.mean(values, axis=-1, keepdims=True)
        shifted = values - center
        spread = jnp.mean(shifted * shifted, axis=-1, keepdims=True)
        normed = (shifted * lax.rsqrt(spread + 1e-05) * gain_ref[...]).astype(jnp.bfloat16)
        normed_ref[j] = normed
        at = jnp.where(line % rows == j, wide, 0.0).astype(jnp.bfloat16)
        acc += lax.dot_general(normed, at, NT, preferred_element_type=jnp.float32)
    bias_ref[...] = acc.astype(jnp.bfloat16)


def normalize(pair, gain, w_bias_t):
    rows, cols, width = pair.shape
    return pl.pallas_call(
        normalize_kernel,
        out_shape=(
            jax.ShapeDtypeStruct((rows, cols, width), jnp.bfloat16),
            jax.ShapeDtypeStruct((cols, 128), jnp.bfloat16),
        ),
        name="normalize",
    )(pair, gain, w_bias_t)


def attend_kernel(
    order_ref, core_ref, *refs
):
    recv_refs, refs = refs[:5], refs[5:]
    own_ref, other_ref, pen_ref, wq_ref, wk_ref, wvt_ref, wg_ref, wo_ref, out_ref, score_bias, folded = refs
    members, rows, cols, width = recv_refs[0].shape
    blocks = sum(ref.shape[0] for ref in recv_refs)
    count = blocks * cols
    here = members * cols
    xs = own_ref.shape[0]
    step = here // (2 * xs)
    lanes = step * HEADS
    first = core_ref[0] == 0

    def lay(k, carry):
        source = pl.ds(pl.multiple_of(order_ref[k] * cols, cols), cols)
        at = pl.ds(pl.multiple_of(k * cols, cols), cols)
        pieces = []
        for x in range(xs):
            own, other = own_ref[x, source, :].astype(jnp.float32), other_ref[x, source, :].astype(jnp.float32)
            pieces.append(jnp.where(first, own, other)[:, :lanes])
            pieces.append(jnp.where(first, other, own)[:, :lanes])
        score_bias[at, :] = jnp.concatenate(pieces, axis=1) + pen_ref[source, :]
        return carry

    lax.fori_loop(0, blocks, lay, 0)

    def one_row(i, carry):
        normed = jnp.concatenate([ref[:, i].reshape(-1, width) for ref in recv_refs], axis=0)
        keys = jnp.dot(normed, wk_ref[...], preferred_element_type=jnp.float32).astype(jnp.bfloat16)
        values_t = lax.dot_general(wvt_ref[...], normed, NT, preferred_element_type=jnp.float32).astype(jnp.bfloat16)
        mine = recv_refs[0][:, i].reshape(here, width)
        query = jnp.dot(mine, wq_ref[...], preferred_element_type=jnp.float32) * HEAD_DIM ** (-0.5)
        query = query.astype(jnp.bfloat16).astype(jnp.float32)
        gate = jax.nn.sigmoid(jnp.dot(mine, wg_ref[...], preferred_element_type=jnp.float32))
        spread = jnp.concatenate(
            [
                jnp.where(head_mask(step, h), query[b * step : (b + 1) * step], 0.0)
                for b in range(here // step)
                for h in range(HEADS)
            ],
            axis=0,
        ).astype(jnp.bfloat16)
        chunk = 256
        for c in range(here * HEADS // chunk):
            at = slice(c * chunk, (c + 1) * chunk)
            scores = lax.dot_general(keys, spread[at], NT, preferred_element_type=jnp.float32) + score_bias[:, at]
            peak = jnp.max(scores, axis=0, keepdims=True)
            weights = jnp.exp(scores - peak)
            total = jnp.sum(weights, axis=0, keepdims=True)
            numer = jnp.dot(values_t, weights.astype(jnp.bfloat16), preferred_element_type=jnp.float32)
            folded[at, :] = (numer / total).T
        attended = jnp.concatenate(
            [
                sum(
                    jnp.where(head_mask(step, h), folded[pl.ds((b * HEADS + h) * step, step), :], 0.0)
                    for h in range(HEADS)
                )
                for b in range(here // step)
            ],
            axis=0,
        )
        gated = (attended * gate).astype(jnp.bfloat16)
        update = jnp.dot(gated, wo_ref[...], preferred_element_type=jnp.float32).astype(jnp.bfloat16)
        out_ref[:, i] = update.reshape(members, cols, width)
        return carry

    lax.fori_loop(0, rows, one_row, 0)


def attend(order, core, recv, own, other, penalty, wq, wk, wvt, wg, wo):
    members, rows, cols, width = recv[0].shape
    here = members * cols
    count = sum(part.shape[0] for part in recv) * cols
    vmem = pl.BlockSpec(memory_space=pltpu.VMEM)
    smem = pl.BlockSpec(memory_space=pltpu.SMEM)
    return pl.pallas_call(
        attend_kernel,
        out_shape=jax.ShapeDtypeStruct((members, rows, cols, width), jnp.bfloat16),
        in_specs=[smem] * 2 + [vmem] * (len(recv) + 8),
        out_specs=vmem,
        scratch_shapes=[
            pltpu.VMEM((count, here * HEADS), jnp.float32),
            pltpu.VMEM((here * HEADS, width), jnp.float32),
        ],
        compiler_params=pltpu.CompilerParams(vmem_limit_bytes=40 * 2**20),
        cost_estimate=pl.CostEstimate(flops=4 * 10**9, bytes_accessed=4 * 10**6, transcendentals=4 * 10**6),
        name="attend",
    )(order, core, *recv, own, other, penalty, wq, wk, wvt, wg, wo)


def gather(block, axes):
    size = lax.axis_size(axes)
    return lax.all_to_all(jnp.broadcast_to(block[None], (size,) + block.shape), axes, 0, 0, tiled=True)


def local(pair, valid, ln_gain, w_query, w_key, w_value, w_gate, w_bias, w_out):
    rows, cols, width = pair.shape
    members = lax.axis_size("yi")
    groups = lax.axis_size(("zh", "yo"))
    core = lax.axis_index("core").astype(jnp.int32).reshape(1)
    group = lax.axis_index(("zh", "yo")).astype(jnp.int32)
    normed, bias = normalize(pair, ln_gain.reshape(1, width), w_bias.T)
    swap = [(a * groups + q, q * groups + a) for a in range(groups) for q in range(groups)]
    bias = lax.ppermute(bias, ("zl", "zh", "yo"), swap)
    flip = [(0, 1), (1, 0)]
    own = lax.all_to_all(normed.reshape(members, rows // members, cols, width), "yi", 0, 0, tiled=True)
    by_z = lax.ppermute(own, "zh", flip)
    by_y = lax.ppermute(own, "yo", flip)
    bias = gather(bias, ("zl", "yi")).reshape(groups * members * cols, 128)
    bias, by_z, by_y = lax.optimization_barrier((bias, by_z, by_y))
    half = members // 2
    far = [lax.ppermute(by_z[:half], "yo", flip), lax.ppermute(by_y[half:], "zh", flip)]
    bias = gather(bias, "x")
    bias, far = lax.optimization_barrier((bias, far))
    other = lax.ppermute(bias, "core", flip)
    penalty = jnp.where(valid == 1, 0.0, -1000000000.0).astype(jnp.float32).reshape(-1, 1)
    order = jnp.concatenate([(group ^ f) * members + jnp.arange(members, dtype=jnp.int32) for f in (0, 2, 1, 3)])
    update = attend(
        order, core, [own, by_z, by_y, *far], bias, other, penalty, w_query, w_key, w_value.T, w_gate, w_out
    )
    update = lax.all_to_all(update, "yi", 0, 0, tiled=True)
    return update.reshape(rows, cols, width)


def solution(mesh):
    fine = Mesh(mesh.devices.reshape(4, 4, 2, 2, 2, 4), ROW + COL)
    return jax.shard_map(
        local,
        mesh=fine,
        in_specs=(P(ROW, COL, None), P(), P(), P(), P(), P(), P(), P(), P()),
        out_specs=P(ROW, COL, None),
        check_vma=False,
    )
```

time: 451 us -> 114 us (0.25)
  the two profiles are of different devices: /device:TPU:1 before, /device:TPU:130 now
where the time goes in v1:
time: 114 us
  starting transfers between devices  53.8 us (47%)
  waiting for transfers between devices  22 us (19%)
  Pallas kernels  17.6 us (15%)
  blocking collectives  17 us (15%)
  local copies, waits for them, and re-layouts  3.28 us (3%)
    all_to_all x2, starting transfers between devices, gather(): lax.all_to_all(jnp.broadcast_to(block[None], (size,) + block.shape), axes...  17.5 us
    all_to_all x1, blocking collectives, local(): update = lax.all_to_all(update, 'yi', 0, 0, tiled=True)  17 us
    pallas_call x1, Pallas kernels, attend(): pl.pallas_call(attend_kernel, out_shape=jax.ShapeDtypeStruct((members, ro...  15 us
    ppermute x1, waiting for transfers between devices, local(): by_z = lax.ppermute(own, 'zh', flip)  10.7 us
    ppermute x1, starting transfers between devices, local(): bias = lax.ppermute(bias, ('zl', 'zh', 'yo'), swap)  7.29 us
    ppermute x1, starting transfers between devices, local(): by_z = lax.ppermute(own, 'zh', flip)  6.11 us
    ppermute x1, starting transfers between devices, local(): lax.ppermute(by_y[half:], 'zh', flip)  5.81 us
    ppermute x1, waiting for transfers between devices, local(): lax.ppermute(by_z[:half], 'yo', flip)  5.8 us
  transfers between devices with their start and end apart: 9, of which 6 were waited for; matrix products, arithmetic and copies ran while one was open for 0% of the time, Pallas kernels for 0%

profile of v1, /device:TPU:130, one launch (start us, length us, event | category | flops | bytes accessed | tf_op | source)
XLA Modules:
  0.0 113.8 jit_solution(2992327065551606823)
XLA Ops:
  0.0 2.5 %normalize.1 = (bf16[24,48,128]{2,1,0:T(8,128)(2,1)}, bf16[48,128]{1,0:T(8,128)(2,1)}) custom-call(bf16[24,48,128]{2,1,0:T(8,128)(2,1)} %pair_ref.1, f32[1,128]{1,0:T(1,128)} %bitcast.12, bf16[4,128]{1,0:T(4,128)(2,1)} %bitcast.11), custom_call_target="tpu_custom_call" | custom-call | tf_op jit(solution)/shard_map/normalize/pallas_call | solution.py:41
  2.5 5.0 %all-to-all-start = ((bf16[4,6,48,128]{3,2,1,0:T(8,128)(2,1)}), bf16[4,6,48,128]{3,2,1,0:T(8,128)(2,1)S(1)}, u32[]{:S(2)}, u32[]{:S(2)}) async-start(bf16[4,6,48,128]{3,2,1,0:T(8,128)(2,1)} %bitcast.10), calls=%async_computation | async-start | bytes 589824 | tf_op jit(solution)/shard_map/all_to_all | solution.py:157
  7.5 7.3 %collective-permute-start = (bf16[48,128]{1,0:T(8,128)(2,1)S(1)}, bf16[48,128]{1,0:T(8,128)(2,1)S(1)}, u32[]{:S(2)}, u32[]{:S(2)}) collective-permute-start(bf16[48,128]{1,0:T(8,128)(2,1)S(1)} %copy-done.6), channel_id=1, source_target_pairs={{0,0},{4,128},{8,256},{12,384},{128,4},{132,132},{136,260},{140,38... | collective-permute-start | bytes 36872 | tf_op jit(solution)/shard_map/ppermute | solution.py:155
  14.8 1.7 %collective-permute-done = bf16[48,128]{1,0:T(8,128)(2,1)S(1)} collective-permute-done((bf16[48,128]{1,0:T(8,128)(2,1)S(1)}, bf16[48,128]{1,0:T(8,128)(2,1)S(1)}, u32[]{:S(2)}, u32[]{:S(2)}) %collective-permute-start) | collective-permute-done | bytes 12320 | tf_op jit(solution)/shard_map/ppermute | solution.py:155
  16.5 0.7 all-to-all-done.refs_0_
  17.1 0.7 broadcast_in_dim.20
  17.8 12.7 %all-to-all-start.1 = ((bf16[16,48,128]{2,1,0:T(8,128)(2,1)}), bf16[16,48,128]{2,1,0:T(8,128)(2,1)S(1)}, u32[]{:S(2)}, u32[]{:S(2)}) async-start(bf16[16,48,128]{2,1,0:T(8,128)(2,1)} %broadcast_in_dim.20), calls=%async_computation.1 | async-start | bytes 393216 | tf_op jit(solution)/shard_map/all_to_all | solution.py:144
  30.5 4.8 %collective-permute-start.2 = (bf16[4,6,48,128]{3,2,1,0:T(8,128)(2,1)S(1)}, bf16[4,6,48,128]{3,2,1,0:T(8,128)(2,1)S(1)}, u32[]{:S(2)}, u32[]{:S(2)}) collective-permute-start(bf16[4,6,48,128]{3,2,1,0:T(8,128)(2,1)S(1)} %all-to-all-done.refs_0_), channel_id=1, source_target_pairs={{0,4},{4,0},{1,5},{5,1},{2,6},{6,2},{3,7},{7,3},{8,12},{12,8},{9,1... | collective-permute-start | bytes 884744 | tf_op jit(solution)/shard_map/ppermute | solution.py:159
  35.4 6.1 %collective-permute-start.1 = (bf16[4,6,48,128]{3,2,1,0:T(8,128)(2,1)S(1)}, bf16[4,6,48,128]{3,2,1,0:T(8,128)(2,1)S(1)}, u32[]{:S(2)}, u32[]{:S(2)}) collective-permute-start(bf16[4,6,48,128]{3,2,1,0:T(8,128)(2,1)S(1)} %all-to-all-done.refs_0_), channel_id=1, source_target_pairs={{0,8},{8,0},{1,9},{9,1},{2,10},{10,2},{3,11},{11,3},{4,12},{12,4},... | collective-permute-start | bytes 884744 | tf_op jit(solution)/shard_map/ppermute | solution.py:158
  41.5 0.0 all-to-all-done.1
  41.5 1.8 %collective-permute-done.2.refs_2_ = bf16[4,6,48,128]{3,2,1,0:T(8,128)(2,1)S(1)} collective-permute-done((bf16[4,6,48,128]{3,2,1,0:T(8,128)(2,1)S(1)}, bf16[4,6,48,128]{3,2,1,0:T(8,128)(2,1)S(1)}, u32[]{:S(2)}, u32[]{:S(2)}) %collective-permute-start.2) | collective-permute-done | bytes 294944 | tf_op jit(solution)/shard_map/ppermute | solution.py:159
  43.3 10.7 %collective-permute-done.1.refs_1_ = bf16[4,6,48,128]{3,2,1,0:T(8,128)(2,1)S(1)} collective-permute-done((bf16[4,6,48,128]{3,2,1,0:T(8,128)(2,1)S(1)}, bf16[4,6,48,128]{3,2,1,0:T(8,128)(2,1)S(1)}, u32[]{:S(2)}, u32[]{:S(2)}) %collective-permute-start.1) | collective-permute-done | bytes 294944 | tf_op jit(solution)/shard_map/ppermute | solution.py:158
  54.1 1.0 broadcast_in_dim.21
  55.1 4.8 %all-to-all-start.2 = ((bf16[4,768,128]{2,1,0:T(8,128)(2,1)}), bf16[4,768,128]{2,1,0:T(8,128)(2,1)S(1)}, u32[]{:S(2)}, u32[]{:S(2)}) async-start(bf16[4,768,128]{2,1,0:T(8,128)(2,1)} %broadcast_in_dim.21), calls=%async_computation.2 | async-start | bytes 1572864 | tf_op jit(solution)/shard_map/all_to_all | solution.py:144
  59.9 0.0 copy-start.4
  59.9 5.8 %collective-permute-start.4 = (bf16[2,6,48,128]{3,2,1,0:T(8,128)(2,1)S(1)}, bf16[2,6,48,128]{3,2,1,0:T(8,128)(2,1)S(1)}, u32[]{:S(2)}, u32[]{:S(2)}) collective-permute-start(bf16[2,6,48,128]{3,2,1,0:T(8,128)(2,1)S(1)} %slice.7), channel_id=1, source_target_pairs={{0,8},{8,0},{1,9},{9,1},{2,10},{10,2},{3,11},{11,3},{4,12},{12,4},... | collective-permute-start | bytes 442376 | tf_op jit(solution)/shard_map/ppermute | solution.py:163
  65.8 5.3 %collective-permute-start.3 = (bf16[2,6,48,128]{3,2,1,0:T(8,128)(2,1)S(1)}, bf16[2,6,48,128]{3,2,1,0:T(8,128)(2,1)S(1)}, u32[]{:S(2)}, u32[]{:S(2)}) collective-permute-start(bf16[2,6,48,128]{3,2,1,0:T(8,128)(2,1)S(1)} %slice.6), channel_id=1, source_target_pairs={{0,4},{4,0},{1,5},{5,1},{2,6},{6,2},{3,7},{7,3},{8,12},{12,8},{9,1... | collective-permute-start | bytes 442376 | tf_op jit(solution)/shard_map/ppermute | solution.py:163
  71.1 0.0 collective-permute-done.4.refs_4_
  71.1 5.8 %collective-permute-done.3.refs_3_ = bf16[2,6,48,128]{3,2,1,0:T(8,128)(2,1)S(1)} collective-permute-done((bf16[2,6,48,128]{3,2,1,0:T(8,128)(2,1)S(1)}, bf16[2,6,48,128]{3,2,1,0:T(8,128)(2,1)S(1)}, u32[]{:S(2)}, u32[]{:S(2)}) %collective-permute-start.3) | collective-permute-done | bytes 147488 | tf_op jit(solution)/shard_map/ppermute | solution.py:163
  76.9 0.0 all-to-all-done.2.refs_5_
  76.9 1.9 %collective-permute-start.5 = (bf16[4,768,128]{2,1,0:T(8,128)(2,1)S(1)}, bf16[4,768,128]{2,1,0:T(8,128)(2,1)S(1)}, u32[]{:S(2)}, u32[]{:S(2)}) collective-permute-start(bf16[4,768,128]{2,1,0:T(8,128)(2,1)S(1)} %all-to-all-done.2.refs_5_), channel_id=1, source_target_pairs={{0,16},{16,0},{1,17},{17,1},{2,18},{18,2},{3,19},{19,3},{4,20},{20... | collective-permute-start | bytes 2359304 | tf_op jit(solution)/shard_map/ppermute | solution.py:166
  78.8 0.0 copy-start.5
  78.9 0.1 copy.11
  79.0 0.6 copy-done.5
  79.5 0.0 copy-start.3
  79.6 0.2 reshape.26.refs_7_
  79.7 0.1 pad_add_fusion.order_ref
  79.8 1.2 %collective-permute-done.5.refs_6_ = bf16[4,768,128]{2,1,0:T(8,128)(2,1)S(1)} collective-permute-done((bf16[4,768,128]{2,1,0:T(8,128)(2,1)S(1)}, bf16[4,768,128]{2,1,0:T(8,128)(2,1)S(1)}, u32[]{:S(2)}, u32[]{:S(2)}) %collective-permute-start.5) | collective-permute-done | bytes 786464 | tf_op jit(solution)/shard_map/ppermute | solution.py:166
  81.1 0.0 copy-done.3
  81.1 15.0 %attend.1 = bf16[4,6,48,128]{3,2,1,0:T(8,128)(2,1)S(1)} custom-call(s32[16]{0:T(128)S(1)} %pad_add_fusion.order_ref, s32[1]{0:T(128)} %bitcast.core_ref, bf16[4,6,48,128]{3,2,1,0:T(8,128)(2,1)S(1)} %all-to-all-done.refs_0_, bf16[4,6,48,128]{3,2,1,0:T(8,128)(2,1)S(1)} %collective-permute-done.1.refs_1_, ...), custom_call_target="tpu_custom_call" | custom-call | flops 4000000000 | bytes 4000000 | tf_op jit(solution)/shard_map/attend/pallas_call | solution.py:127
  96.1 17.0 %all_to_all.20 = bf16[4,6,48,128]{3,2,1,0:T(8,128)(2,1)S(1)} all-to-all(bf16[4,6,48,128]{3,2,1,0:T(8,128)(2,1)S(1)} %attend.1), channel_id=1, replica_groups=mesh['zl'=4,'x'=4,'core'=2,'zh'=2,'yo'=2,'yi'=4] {'yi'}, dimensions={0} | all-to-all | bytes 589824 | tf_op jit(solution)/shard_map/all_to_all | solution.py:172
  113.1 0.7 copy.14
  (14 shorter events, 0.1 us)
Async XLA Ops:
  2.5 5.0 %copy-start.6 = (bf16[48,128]{1,0:T(8,128)(2,1)S(1)}, bf16[48,128]{1,0:T(8,128)(2,1)}, u32[]{:S(2)}) copy-start(bf16[48,128]{1,0:T(8,128)(2,1)} %get-tuple-element.14) | copy-start | bytes 36868
  2.5 14.6 %all-to-all-start = ((bf16[4,6,48,128]{3,2,1,0:T(8,128)(2,1)}), bf16[4,6,48,128]{3,2,1,0:T(8,128)(2,1)S(1)}, u32[]{:S(2)}, u32[]{:S(2)}) async-start(bf16[4,6,48,128]{3,2,1,0:T(8,128)(2,1)} %bitcast.10), calls=%async_computation | async-start | bytes 589824 | tf_op jit(solution)/shard_map/all_to_all | solution.py:157
  7.5 9.0 %collective-permute-start = (bf16[48,128]{1,0:T(8,128)(2,1)S(1)}, bf16[48,128]{1,0:T(8,128)(2,1)S(1)}, u32[]{:S(2)}, u32[]{:S(2)}) collective-permute-start(bf16[48,128]{1,0:T(8,128)(2,1)S(1)} %copy-done.6), channel_id=1, source_target_pairs={{0,0},{4,128},{8,256},{12,384},{128,4},{132,132},{136,260},{140,38... | collective-permute-start | bytes 36872 | tf_op jit(solution)/shard_map/ppermute | solution.py:155
  17.8 23.7 %all-to-all-start.1 = ((bf16[16,48,128]{2,1,0:T(8,128)(2,1)}), bf16[16,48,128]{2,1,0:T(8,128)(2,1)S(1)}, u32[]{:S(2)}, u32[]{:S(2)}) async-start(bf16[16,48,128]{2,1,0:T(8,128)(2,1)} %broadcast_in_dim.20), calls=%async_computation.1 | async-start | bytes 393216 | tf_op jit(solution)/shard_map/all_to_all | solution.py:144
  30.5 12.8 %collective-permute-start.2 = (bf16[4,6,48,128]{3,2,1,0:T(8,128)(2,1)S(1)}, bf16[4,6,48,128]{3,2,1,0:T(8,128)(2,1)S(1)}, u32[]{:S(2)}, u32[]{:S(2)}) collective-permute-start(bf16[4,6,48,128]{3,2,1,0:T(8,128)(2,1)S(1)} %all-to-all-done.refs_0_), channel_id=1, source_target_pairs={{0,4},{4,0},{1,5},{5,1},{2,6},{6,2},{3,7},{7,3},{8,12},{12,8},{9,1... | collective-permute-start | bytes 884744 | tf_op jit(solution)/shard_map/ppermute | solution.py:159
  35.4 18.7 %collective-permute-start.1 = (bf16[4,6,48,128]{3,2,1,0:T(8,128)(2,1)S(1)}, bf16[4,6,48,128]{3,2,1,0:T(8,128)(2,1)S(1)}, u32[]{:S(2)}, u32[]{:S(2)}) collective-permute-start(bf16[4,6,48,128]{3,2,1,0:T(8,128)(2,1)S(1)} %all-to-all-done.refs_0_), channel_id=1, source_target_pairs={{0,8},{8,0},{1,9},{9,1},{2,10},{10,2},{3,11},{11,3},{4,12},{12,4},... | collective-permute-start | bytes 884744 | tf_op jit(solution)/shard_map/ppermute | solution.py:158
  55.1 21.8 %all-to-all-start.2 = ((bf16[4,768,128]{2,1,0:T(8,128)(2,1)}), bf16[4,768,128]{2,1,0:T(8,128)(2,1)S(1)}, u32[]{:S(2)}, u32[]{:S(2)}) async-start(bf16[4,768,128]{2,1,0:T(8,128)(2,1)} %broadcast_in_dim.21), calls=%async_computation.2 | async-start | bytes 1572864 | tf_op jit(solution)/shard_map/all_to_all | solution.py:144
  59.9 18.9 %copy-start.4 = (bf16[128,128]{1,0:T(8,128)(2,1)S(1)}, bf16[128,128]{1,0:T(8,128)(2,1)}, u32[]{:S(2)}) copy-start(bf16[128,128]{1,0:T(8,128)(2,1)} %param.14) | copy-start | bytes 98308
  59.9 11.1 %collective-permute-start.4 = (bf16[2,6,48,128]{3,2,1,0:T(8,128)(2,1)S(1)}, bf16[2,6,48,128]{3,2,1,0:T(8,128)(2,1)S(1)}, u32[]{:S(2)}, u32[]{:S(2)}) collective-permute-start(bf16[2,6,48,128]{3,2,1,0:T(8,128)(2,1)S(1)} %slice.7), channel_id=1, source_target_pairs={{0,8},{8,0},{1,9},{9,1},{2,10},{10,2},{3,11},{11,3},{4,12},{12,4},... | collective-permute-start | bytes 442376 | tf_op jit(solution)/shard_map/ppermute | solution.py:163
  65.8 11.1 %collective-permute-start.3 = (bf16[2,6,48,128]{3,2,1,0:T(8,128)(2,1)S(1)}, bf16[2,6,48,128]{3,2,1,0:T(8,128)(2,1)S(1)}, u32[]{:S(2)}, u32[]{:S(2)}) collective-permute-start(bf16[2,6,48,128]{3,2,1,0:T(8,128)(2,1)S(1)} %slice.6), channel_id=1, source_target_pairs={{0,4},{4,0},{1,5},{5,1},{2,6},{6,2},{3,7},{7,3},{8,12},{12,8},{9,1... | collective-permute-start | bytes 442376 | tf_op jit(solution)/shard_map/ppermute | solution.py:163
  76.9 4.2 %collective-permute-start.5 = (bf16[4,768,128]{2,1,0:T(8,128)(2,1)S(1)}, bf16[4,768,128]{2,1,0:T(8,128)(2,1)S(1)}, u32[]{:S(2)}, u32[]{:S(2)}) collective-permute-start(bf16[4,768,128]{2,1,0:T(8,128)(2,1)S(1)} %all-to-all-done.2.refs_5_), channel_id=1, source_target_pairs={{0,16},{16,0},{1,17},{17,1},{2,18},{18,2},{3,19},{19,3},{4,20},{20... | collective-permute-start | bytes 2359304 | tf_op jit(solution)/shard_map/ppermute | solution.py:166
  78.8 0.7 copy-start.5
  79.5 1.5 %copy-start = (bf16[128,128]{1,0:T(8,128)(2,1)S(1)}, bf16[128,128]{1,0:T(8,128)(2,1)}, u32[]{:S(2)}) copy-start(bf16[128,128]{1,0:T(8,128)(2,1)} %refs_8_.1) | copy-start | bytes 98308
  79.5 1.5 %copy-start.1 = (bf16[128,128]{1,0:T(8,128)(2,1)S(1)}, bf16[128,128]{1,0:T(8,128)(2,1)}, u32[]{:S(2)}) copy-start(bf16[128,128]{1,0:T(8,128)(2,1)} %refs_9_.1) | copy-start | bytes 98308
  79.5 1.5 %copy-start.2 = (bf16[128,128]{1,0:T(8,128)(2,1)S(1)}, bf16[128,128]{1,0:T(8,128)(2,1)}, u32[]{:S(2)}) copy-start(bf16[128,128]{1,0:T(8,128)(2,1)} %refs_11_.1) | copy-start | bytes 98308
  79.5 1.5 %copy-start.3 = (bf16[128,128]{1,0:T(8,128)(2,1)S(1)}, bf16[128,128]{1,0:T(8,128)(2,1)}, u32[]{:S(2)}) copy-start(bf16[128,128]{1,0:T(8,128)(2,1)} %refs_12_.1) | copy-start | bytes 98308

commit v2 on v1

v2 whole, which is shorter than its diff:
```python
import functools

import jax
import jax.numpy as jnp
from jax import lax
from jax.experimental import pallas as pl
from jax.experimental.pallas import tpu as pltpu
from jax.sharding import Mesh
from jax.sharding import PartitionSpec as P

HEADS = 4
HEAD_DIM = 32
ROW = ("zl1", "zl0", "x", "core")
COL = ("zh", "y")
NT = (((1,), (1,)), ((), ()))


def head_mask(rows, h):
    lane = lax.broadcasted_iota(jnp.int32, (rows, 128), 1)
    return lane // HEAD_DIM == h


def normalize_kernel(pair_ref, gain_ref, w_ref, sent_ref):
    rows, cols, width = pair_ref.shape
    peers, per = sent_ref.shape[0], sent_ref.shape[1] - 1
    line = lax.broadcasted_iota(jnp.int32, (128, width), 0)
    w_t = w_ref[...].astype(jnp.float32)
    wide = sum(jnp.where(line // rows == h, w_t[h : h + 1, :], 0.0) for h in range(HEADS))
    acc = jnp.zeros((cols, 128), jnp.float32)
    for j in range(rows):
        values = pair_ref[j].astype(jnp.float32)
        center = jnp.mean(values, axis=-1, keepdims=True)
        shifted = values - center
        spread = jnp.mean(shifted * shifted, axis=-1, keepdims=True)
        normed = (shifted * lax.rsqrt(spread + 1e-05) * gain_ref[...]).astype(jnp.bfloat16)
        sent_ref[j // per, j % per] = normed
        at = jnp.where(line % rows == j, wide, 0.0).astype(jnp.bfloat16)
        acc += lax.dot_general(normed, at, NT, preferred_element_type=jnp.float32)
    bias = acc.astype(jnp.bfloat16)
    for peer in range(peers):
        sent_ref[peer, per] = bias


def normalize(pair, gain, w_bias_t, peers):
    rows, cols, width = pair.shape
    return pl.pallas_call(
        normalize_kernel,
        out_shape=jax.ShapeDtypeStruct((peers, rows // peers + 1, cols, width), jnp.bfloat16),
        name="normalize",
    )(pair, gain, w_bias_t)


def project_kernel(own_ref, far_ref, wq_ref, wk_ref, wvt_ref, wg_ref, key_ref, value_ref, query_ref, gate_ref):
    blocks, rows, cols, width = own_ref.shape
    step = cols // 2
    masks = [head_mask(step, h) for h in range(HEADS)]
    for i in range(rows):
        own = own_ref[:, i].reshape(blocks * cols, width)
        normed = jnp.concatenate([own, far_ref[:, i].reshape(blocks * cols, width)], axis=0)
        key_ref[i] = jnp.dot(normed, wk_ref[...], preferred_element_type=jnp.float32).astype(jnp.bfloat16)
        value_ref[i] = lax.dot_general(wvt_ref[...], normed, NT, preferred_element_type=jnp.float32).astype(
            jnp.bfloat16
        )
        query = jnp.dot(own, wq_ref[...], preferred_element_type=jnp.float32) * HEAD_DIM ** (-0.5)
        query = query.astype(jnp.bfloat16).astype(jnp.float32)
        gate = jax.nn.sigmoid(jnp.dot(own, wg_ref[...], preferred_element_type=jnp.float32))
        for half in range(2):
            starts = [b * cols + half * step for b in range(blocks)]
            query_ref[half, i] = jnp.concatenate(
                [jnp.where(masks[h], query[at : at + step], 0.0) for at in starts for h in range(HEADS)], axis=0
            ).astype(jnp.bfloat16)
            gate_ref[half, i] = jnp.concatenate([gate[at : at + step] for at in starts], axis=0)


def project(own, far, wq, wk, wvt, wg):
    blocks, rows, cols, width = own.shape
    count = 2 * blocks * cols
    return pl.pallas_call(
        project_kernel,
        out_shape=(
            jax.ShapeDtypeStruct((rows, count, width), jnp.bfloat16),
            jax.ShapeDtypeStruct((rows, width, count), jnp.bfloat16),
            jax.ShapeDtypeStruct((2, rows, count // 4 * HEADS, width), jnp.bfloat16),
            jax.ShapeDtypeStruct((2, rows, count // 4, width), jnp.float32),
        ),
        compiler_params=pltpu.CompilerParams(vmem_limit_bytes=16 * 2**20),
        cost_estimate=pl.CostEstimate(flops=10**9, bytes_accessed=10**7, transcendentals=10**6),
        name="project",
    )(own, far, wq, wk, wvt, wg)


def attend_kernel(
    first, half_ref, bias_ref, pen_ref, key_ref, value_ref, query_ref, gate_ref, wo_ref, *refs
):
    before_ref, out_ref, score_bias, folded = (None, *refs) if first else refs
    blocks, rows, _, width = out_ref.shape
    count = key_ref.shape[1]
    lanes = query_ref.shape[2] // blocks
    step = lanes // HEADS
    here = blocks * step
    quarter = bias_ref.shape[2]
    part, chunk = 48, 128
    half = half_ref[0]
    masks = [head_mask(step, h) for h in range(HEADS)]

    for k in range(0, count, part):
        z, m, at = k // (HEADS * quarter), k // quarter % HEADS, k % quarter
        pieces = [
            bias_ref[b, z, at : at + part, m * lanes : (m + 1) * lanes].astype(jnp.float32) for b in range(blocks)
        ]
        score_bias[k : k + part, :] = jnp.concatenate(pieces, axis=1) + pen_ref[k : k + part, :]

    for i in range(rows):
        for c in range(0, blocks * lanes, chunk):
            at = slice(c, c + chunk)
            scores = lax.dot_general(key_ref[i], query_ref[half, i, at, :], NT, preferred_element_type=jnp.float32)
            scores = scores + score_bias[:, at]
            peak = jnp.max(scores, axis=0, keepdims=True)
            weights = jnp.exp(scores - peak)
            total = jnp.sum(weights, axis=0, keepdims=True)
            numer = jnp.dot(value_ref[i], weights.astype(jnp.bfloat16), preferred_element_type=jnp.float32)
            folded[i, at, :] = (numer * (1.0 / total)).T

    gated = []
    for i in range(rows):
        attended = [
            sum(
                jnp.where(masks[h], folded[i, (b * HEADS + h) * step : (b * HEADS + h + 1) * step, :], 0.0)
                for h in range(HEADS)
            )
            for b in range(blocks)
        ]
        gated.append((jnp.concatenate(attended, axis=0) * gate_ref[half, i]).astype(jnp.bfloat16))
    update = jnp.dot(jnp.concatenate(gated, axis=0), wo_ref[...], preferred_element_type=jnp.float32)
    for i in range(rows):
        for b in range(blocks):
            mine = update[i * here + b * step : i * here + (b + 1) * step]
            if first:
                out_ref[b, i] = mine
            else:
                other = before_ref[b, i]
                joined = [jnp.where(half == 0, mine, other), jnp.where(half == 0, other, mine)]
                out_ref[b, i] = jnp.concatenate(joined, axis=0).astype(jnp.bfloat16)


def attend(half, bias, penalty, keys, values, query, gate, wo, before=None):
    blocks = bias.shape[0]
    rows, count, width = keys.shape
    here = query.shape[2]
    step = here // HEADS // blocks
    vmem = pl.BlockSpec(memory_space=pltpu.VMEM)
    smem = pl.BlockSpec(memory_space=pltpu.SMEM)
    if before is None:
        out, more = jax.ShapeDtypeStruct((blocks, rows, step, width), jnp.float32), ()
    else:
        out, more = jax.ShapeDtypeStruct((blocks, rows, 2 * step, width), jnp.bfloat16), (before,)
    return pl.pallas_call(
        functools.partial(attend_kernel, before is None),
        out_shape=out,
        in_specs=[smem] + [vmem] * (7 + len(more)),
        out_specs=vmem,
        scratch_shapes=[pltpu.VMEM((count, here), jnp.float32), pltpu.VMEM((rows, here, width), jnp.float32)],
        compiler_params=pltpu.CompilerParams(vmem_limit_bytes=16 * 2**20),
        cost_estimate=pl.CostEstimate(flops=2 * 10**9, bytes_accessed=2 * 10**7, transcendentals=2 * 10**6),
        name="attend",
    )(half, bias, penalty, keys, values, query, gate, wo, *more)


def gather(block, axes):
    size = lax.axis_size(axes)
    return lax.all_to_all(jnp.broadcast_to(block[None], (size,) + block.shape), axes, 0, 0, tiled=True)


def local(pair, valid, ln_gain, w_query, w_key, w_value, w_gate, w_bias, w_out):
    rows, cols, width = pair.shape
    ring = lax.axis_size("y")
    core = lax.axis_index("core").astype(jnp.int32).reshape(1)
    first_z = lax.axis_index("zh") == 0
    flip = [(0, 1), (1, 0)]
    got = lax.all_to_all(normalize(pair, ln_gain.reshape(1, width), w_bias.T, ring), "y", 0, 0, tiled=True)
    bias = got[:, -1].reshape(HEADS, -1, 128)
    bias = jnp.concatenate([bias[m, :, : rows * HEADS] for m in range(HEADS)], axis=1)
    same = lax.ppermute(bias, ("zl1", "zh"), [(0, 0), (1, 2), (2, 1), (3, 3)])
    swap = lax.ppermute(bias, ("zl1", "zh"), [(0, 2), (1, 0), (2, 3), (3, 1)])
    straight = lax.axis_index("zl1") == lax.axis_index("zh")
    bias = jnp.stack([jnp.where(straight, same, swap), jnp.where(straight, swap, same)])
    bias, near = lax.optimization_barrier((bias, got[:, :-1]))
    far = lax.ppermute(near, "zh", flip)
    bias = gather(bias, ("zl0", "x"))
    bias, far = lax.optimization_barrier((bias, far))
    other = lax.ppermute(bias, "core", flip)
    penalty = jnp.where(valid == 1, 0.0, -1000000000.0).astype(jnp.float32).reshape(2, -1)
    penalty = jnp.where(first_z, penalty, penalty[::-1]).reshape(-1, 1)
    parts = project(near, far, w_query, w_key, w_value.T, w_gate)
    update = attend(core, bias, penalty, *parts, w_out)
    update = attend(1 - core, other, penalty, *parts, w_out, update)
    return lax.all_to_all(update, "y", 0, 0, tiled=True).reshape(rows, cols, width)


def solution(mesh):
    fine = Mesh(mesh.devices.reshape(2, 2, 4, 2, 2, 8), ROW + COL)
    return jax.shard_map(
        local,
        mesh=fine,
        in_specs=(P(ROW, COL, None), P(), P(), P(), P(), P(), P(), P(), P()),
        out_specs=P(ROW, COL, None),
        check_vma=False,
    )
```

time: 114 us -> 102 us (0.89)
  starting transfers between devices: 53.8 us -> 23 us
  blocking collectives: 17 us -> 38.8 us
  Pallas kernels: 17.6 us -> 10.6 us
  waiting for transfers between devices: 22 us -> 26.3 us
    all_to_all x1 -> x2, blocking collectives: 17 us -> 38.8 us  [the longest x1 21.8 us: local(): lax.all_to_all(normalize(pair, ln_gain.reshape(1, width), w_bias.T, ring)...]
    ppermute x5 -> x3, starting transfers between devices: 29.4 us -> 14.5 us  [the longest x1 7.3 us: local(): same = lax.ppermute(bias, ('zl1', 'zh'), [(0, 0), (1, 2), (2, 1), (3, 3)])]
    all_to_all x2 -> x1, starting transfers between devices: 17.5 us -> 6.58 us  [gather(): lax.all_to_all(jnp.broadcast_to(block[None], (size,) + block.shape), axes...]
    pallas_call x2 -> x4, Pallas kernels: 17.6 us -> 10.6 us  [the longest x2 7.29 us: attend(): pl.pallas_call(functools.partial(attend_kernel, before is None), out_shap...]
    ppermute x5 -> x3, waiting for transfers between devices: 20.1 us -> 26.2 us  [the longest x1 21.6 us: local(): far = lax.ppermute(near, 'zh', flip)]
    all_to_all x1 -> x0, starting transfers between devices: 5 us -> none  [local(): lax.all_to_all(normed.reshape(members, rows // members, cols, width), 'yi...]
    ppermute x1, waiting for transfers between devices: 1.24 us -> 0.01 us  [local(): other = lax.ppermute(bias, 'core', flip)]
  transfers between devices with their start and end apart: 9 -> 5, of which waited for: 6 -> 3; matrix products, arithmetic and copies ran while one was open for 0% -> 0% of each run, Pallas kernels for 0% -> 4%
where the time goes in v2:
time: 102 us; the launch traced here: 101 us
  blocking collectives  38.8 us (38%)
  waiting for transfers between devices  26.3 us (26%)
  starting transfers between devices  23 us (23%)
  Pallas kernels  10.6 us (10%)
  local copies, waits for them, and re-layouts  2.48 us (2%)
    all_to_all x1, blocking collectives, local(): lax.all_to_all(normalize(pair, ln_gain.reshape(1, width), w_bias.T, ring)...  21.8 us
    ppermute x1, waiting for transfers between devices, local(): far = lax.ppermute(near, 'zh', flip)  21.6 us
    all_to_all x1, blocking collectives, local(): lax.all_to_all(update, 'y', 0, 0, tiled=True).reshape(rows, cols, width)  17.1 us
    ppermute x1, starting transfers between devices, local(): same = lax.ppermute(bias, ('zl1', 'zh'), [(0, 0), (1, 2), (2, 1), (3, 3)])  7.3 us
    pallas_call x2, Pallas kernels, attend(): pl.pallas_call(functools.partial(attend_kernel, before is None), out_shap...  7.29 us
    all_to_all x1, starting transfers between devices, gather(): lax.all_to_all(jnp.broadcast_to(block[None], (size,) + block.shape), axes...  6.58 us
    ppermute x1, starting transfers between devices, local(): far = lax.ppermute(near, 'zh', flip)  4.7 us
    ppermute x1, waiting for transfers between devices, local(): swap = lax.ppermute(bias, ('zl1', 'zh'), [(0, 2), (1, 0), (2, 3), (3, 1)])  3.59 us
  transfers between devices with their start and end apart: 5, of which 3 were waited for; matrix products, arithmetic and copies ran while one was open for 0% of the time, Pallas kernels for 4%

profile of v2, /device:TPU:130, one launch (start us, length us, event | category | flops | bytes accessed | tf_op | source)
XLA Modules:
  0.0 101.5 jit_solution(10917189545063956378)
XLA Ops:
  0.0 2.6 %normalize.1 = bf16[8,4,48,128]{3,2,1,0:T(8,128)(2,1)} custom-call(bf16[24,48,128]{2,1,0:T(8,128)(2,1)} %pair_ref.1, f32[1,128]{1,0:T(1,128)} %bitcast.30, bf16[4,128]{1,0:T(4,128)(2,1)} %bitcast.29), custom_call_target="tpu_custom_call" | custom-call | tf_op jit(solution)/shard_map/normalize/pallas_call | solution.py:46
  2.6 21.8 %all_to_all.15 = bf16[8,4,48,128]{3,2,1,0:T(8,128)(2,1)S(1)} all-to-all(bf16[8,4,48,128]{3,2,1,0:T(8,128)(2,1)} %normalize.1), channel_id=1, replica_groups=mesh['zl1'=2,'zl0'=2,'x'=4,'core'=2,'zh'=2,'y'=8] {'y'}, dimensions={0} | all-to-all | bytes 786432 | tf_op jit(solution)/shard_map/all_to_all | solution.py:180
  24.5 0.1 pad_maximum_fusion.1
  24.6 7.3 %collective-permute-start = (bf16[96,384]{1,0:T(8,128)(2,1)S(1)}, bf16[96,384]{1,0:T(8,128)(2,1)S(1)}, u32[]{:S(2)}, u32[]{:S(2)}) collective-permute-start(bf16[96,384]{1,0:T(8,128)(2,1)S(1)} %pad_maximum_fusion.1), channel_id=1, source_target_pairs={{0,0},{8,256},{256,8},{264,264},{1,1},{9,257},{257,9},{265,265},{2... | collective-permute-start | bytes 221192 | tf_op jit(solution)/shard_map/ppermute | solution.py:183
  31.9 2.5 %collective-permute-start.1 = (bf16[96,384]{1,0:T(8,128)(2,1)S(1)}, bf16[96,384]{1,0:T(8,128)(2,1)S(1)}, u32[]{:S(2)}, u32[]{:S(2)}) collective-permute-start(bf16[96,384]{1,0:T(8,128)(2,1)S(1)} %pad_maximum_fusion.1), channel_id=1, source_target_pairs={{0,256},{8,0},{256,264},{264,8},{1,257},{9,1},{257,265},{265,9},{2... | collective-permute-start | bytes 221192 | tf_op jit(solution)/shard_map/ppermute | solution.py:184
  34.4 1.1 %collective-permute-done = bf16[96,384]{1,0:T(8,128)(2,1)S(1)} collective-permute-done((bf16[96,384]{1,0:T(8,128)(2,1)S(1)}, bf16[96,384]{1,0:T(8,128)(2,1)S(1)}, u32[]{:S(2)}, u32[]{:S(2)}) %collective-permute-start) | collective-permute-done | bytes 73760 | tf_op jit(solution)/shard_map/ppermute | solution.py:183
  35.5 3.6 %collective-permute-done.1 = bf16[96,384]{1,0:T(8,128)(2,1)S(1)} collective-permute-done((bf16[96,384]{1,0:T(8,128)(2,1)S(1)}, bf16[96,384]{1,0:T(8,128)(2,1)S(1)}, u32[]{:S(2)}, u32[]{:S(2)}) %collective-permute-start.1) | collective-permute-done | bytes 73760 | tf_op jit(solution)/shard_map/ppermute | solution.py:184
  39.2 1.2 %broadcast_in_dim.14 = bf16[8,2,96,384]{3,2,1,0:T(8,128)(2,1)} broadcast(bf16[2,96,384]{2,1,0:T(8,128)(2,1)S(1)} %pad_maximum_fusion), dimensions={1,2,3} | broadcast | bytes 1327104 | tf_op jit(solution)/shard_map/broadcast_in_dim | solution.py:171
  40.3 0.0 copy-start.4
  40.3 0.0 copy-start.5
  40.3 0.0 copy-start.2
  40.4 6.6 %all-to-all-start.1 = ((bf16[8,2,96,384]{3,2,1,0:T(8,128)(2,1)}), bf16[8,2,96,384]{3,2,1,0:T(8,128)(2,1)S(1)}, u32[]{:S(2)}, u32[]{:S(2)}) async-start(bf16[8,2,96,384]{3,2,1,0:T(8,128)(2,1)} %broadcast_in_dim.14), calls=%async_computation.1 | async-start | bytes 2359296 | tf_op jit(solution)/shard_map/all_to_all | solution.py:171
  46.9 4.7 %collective-permute-start.2 = (bf16[8,3,48,128]{3,2,1,0:T(8,128)(2,1)S(1)}, bf16[8,3,48,128]{3,2,1,0:T(8,128)(2,1)S(1)}, u32[]{:S(2)}, u32[]{:S(2)}) collective-permute-start(bf16[8,3,48,128]{3,2,1,0:T(8,128)(2,1)S(1)} %slice.29.own_ref), channel_id=1, source_target_pairs={{0,8},{8,0},{1,9},{9,1},{2,10},{10,2},{3,11},{11,3},{4,12},{12,4},... | collective-permute-start | bytes 884744 | tf_op jit(solution)/shard_map/ppermute | solution.py:188
  51.6 21.6 %collective-permute-done.2.far_ref = bf16[8,3,48,128]{3,2,1,0:T(8,128)(2,1)S(1)} collective-permute-done((bf16[8,3,48,128]{3,2,1,0:T(8,128)(2,1)S(1)}, bf16[8,3,48,128]{3,2,1,0:T(8,128)(2,1)S(1)}, u32[]{:S(2)}, u32[]{:S(2)}) %collective-permute-start.2) | collective-permute-done | bytes 294944 | tf_op jit(solution)/shard_map/ppermute | solution.py:188
  73.2 0.0 all-to-all-done.1.bias_ref
  73.2 1.9 %collective-permute-start.3 = (bf16[8,2,96,384]{3,2,1,0:T(8,128)(2,1)S(1)}, bf16[8,2,96,384]{3,2,1,0:T(8,128)(2,1)S(1)}, u32[]{:S(2)}, u32[]{:S(2)}) collective-permute-start(bf16[8,2,96,384]{3,2,1,0:T(8,128)(2,1)S(1)} %all-to-all-done.1.bias_ref), channel_id=1, source_target_pairs={{0,16},{16,0},{1,17},{17,1},{2,18},{18,2},{3,19},{19,3},{4,20},{20... | collective-permute-start | bytes 3538952 | tf_op jit(solution)/shard_map/ppermute | solution.py:191
  75.1 0.0 copy-done.4
  75.1 0.1 copy.11
  75.2 0.0 copy-done.5
  75.3 0.1 rev.3
  75.4 0.2 copy.15
  75.6 0.0 copy-done
  75.6 0.0 copy-done.1
  75.6 0.0 copy-done.2
  75.6 0.0 copy-start.3
  75.7 0.6 project.1
  76.3 0.1 copy-done.3
  76.4 3.6 %attend.2.refs_0_ = f32[8,3,24,128]{3,2,1,0:T(8,128)S(1)} custom-call(s32[1]{0:T(128)} %bitcast.half_ref, bf16[8,2,96,384]{3,2,1,0:T(8,128)(2,1)S(1)} %all-to-all-done.1.bias_ref, f32[768,1]{1,0:T(8,128)S(1)} %bitcast.23, bf16[3,768,128]{2,1,0:T(8,128)(2,1)S(1)} %get-tuple-element.17.key_ref, bf16[3,128,768]{2,1,0:T(8,128)(2,1)S(1)} %get-tuple-element.18.value_ref, ...), custom_call_target="tpu_custom_call" | custom-call | flops 2000000000 | bytes 20000000 | tf_op jit(solution)/shard_map/attend/pallas_call | solution.py:157
  80.1 0.0 collective-permute-done.3.bias_ref
  80.1 3.6 %attend.3 = bf16[8,3,48,128]{3,2,1,0:T(8,128)(2,1)S(1)} custom-call(s32[1]{0:T(128)S(6)} %sub.3.half_ref, bf16[8,2,96,384]{3,2,1,0:T(8,128)(2,1)S(1)} %collective-permute-done.3.bias_ref, f32[768,1]{1,0:T(8,128)S(1)} %bitcast.24, bf16[3,768,128]{2,1,0:T(8,128)(2,1)S(1)} %get-tuple-element.17.key_ref, bf16[3,128,768]{2,1,0:T(8,128)(2,1)S(1)} %get-tuple-element.18.value_ref, ...), custom_call_target="tpu_custom_call" | custom-call | flops 2000000000 | bytes 20000000 | tf_op jit(solution)/shard_map/attend/pallas_call | solution.py:157
  83.7 17.1 %all_to_all.16 = bf16[8,3,48,128]{3,2,1,0:T(8,128)(2,1)S(1)} all-to-all(bf16[8,3,48,128]{3,2,1,0:T(8,128)(2,1)S(1)} %attend.3), channel_id=1, replica_groups=mesh['zl1'=2,'zl0'=2,'x'=4,'core'=2,'zh'=2,'y'=8] {'y'}, dimensions={0} | all-to-all | bytes 589824 | tf_op jit(solution)/shard_map/all_to_all | solution.py:197
  100.8 0.7 copy.17
  (11 shorter events, 0.1 us)
Async XLA Ops:
  24.6 10.9 %collective-permute-start = (bf16[96,384]{1,0:T(8,128)(2,1)S(1)}, bf16[96,384]{1,0:T(8,128)(2,1)S(1)}, u32[]{:S(2)}, u32[]{:S(2)}) collective-permute-start(bf16[96,384]{1,0:T(8,128)(2,1)S(1)} %pad_maximum_fusion.1), channel_id=1, source_target_pairs={{0,0},{8,256},{256,8},{264,264},{1,1},{9,257},{257,9},{265,265},{2... | collective-permute-start | bytes 221192 | tf_op jit(solution)/shard_map/ppermute | solution.py:183
  31.9 7.2 %collective-permute-start.1 = (bf16[96,384]{1,0:T(8,128)(2,1)S(1)}, bf16[96,384]{1,0:T(8,128)(2,1)S(1)}, u32[]{:S(2)}, u32[]{:S(2)}) collective-permute-start(bf16[96,384]{1,0:T(8,128)(2,1)S(1)} %pad_maximum_fusion.1), channel_id=1, source_target_pairs={{0,256},{8,0},{256,264},{264,8},{1,257},{9,1},{257,265},{265,9},{2... | collective-permute-start | bytes 221192 | tf_op jit(solution)/shard_map/ppermute | solution.py:184
  40.3 34.8 %copy-start.4 = (bf16[128,128]{1,0:T(8,128)(2,1)S(1)}, bf16[128,128]{1,0:T(8,128)(2,1)}, u32[]{:S(2)}) copy-start(bf16[128,128]{1,0:T(8,128)(2,1)} %param.14) | copy-start | bytes 98308
  40.3 34.9 %copy-start.5 = (s32[768]{0:T(1024)S(1)}, s32[768]{0:T(1024)}, u32[]{:S(2)}) copy-start(s32[768]{0:T(1024)} %param.10) | copy-start | bytes 9220
  40.3 35.3 %copy-start = (bf16[128,128]{1,0:T(8,128)(2,1)S(1)}, bf16[128,128]{1,0:T(8,128)(2,1)}, u32[]{:S(2)}) copy-start(bf16[128,128]{1,0:T(8,128)(2,1)} %wq_ref.1) | copy-start | bytes 98308
  40.3 35.3 %copy-start.1 = (bf16[128,128]{1,0:T(8,128)(2,1)S(1)}, bf16[128,128]{1,0:T(8,128)(2,1)}, u32[]{:S(2)}) copy-start(bf16[128,128]{1,0:T(8,128)(2,1)} %wk_ref.1) | copy-start | bytes 98308
  40.3 35.3 %copy-start.2 = (bf16[128,128]{1,0:T(8,128)(2,1)S(1)}, bf16[128,128]{1,0:T(8,128)(2,1)}, u32[]{:S(2)}) copy-start(bf16[128,128]{1,0:T(8,128)(2,1)} %wg_ref.1) | copy-start | bytes 98308
  40.4 32.8 %all-to-all-start.1 = ((bf16[8,2,96,384]{3,2,1,0:T(8,128)(2,1)}), bf16[8,2,96,384]{3,2,1,0:T(8,128)(2,1)S(1)}, u32[]{:S(2)}, u32[]{:S(2)}) async-start(bf16[8,2,96,384]{3,2,1,0:T(8,128)(2,1)} %broadcast_in_dim.14), calls=%async_computation.1 | async-start | bytes 2359296 | tf_op jit(solution)/shard_map/all_to_all | solution.py:171
  46.9 26.3 %collective-permute-start.2 = (bf16[8,3,48,128]{3,2,1,0:T(8,128)(2,1)S(1)}, bf16[8,3,48,128]{3,2,1,0:T(8,128)(2,1)S(1)}, u32[]{:S(2)}, u32[]{:S(2)}) collective-permute-start(bf16[8,3,48,128]{3,2,1,0:T(8,128)(2,1)S(1)} %slice.29.own_ref), channel_id=1, source_target_pairs={{0,8},{8,0},{1,9},{9,1},{2,10},{10,2},{3,11},{11,3},{4,12},{12,4},... | collective-permute-start | bytes 884744 | tf_op jit(solution)/shard_map/ppermute | solution.py:188
  73.2 6.9 %collective-permute-start.3 = (bf16[8,2,96,384]{3,2,1,0:T(8,128)(2,1)S(1)}, bf16[8,2,96,384]{3,2,1,0:T(8,128)(2,1)S(1)}, u32[]{:S(2)}, u32[]{:S(2)}) collective-permute-start(bf16[8,2,96,384]{3,2,1,0:T(8,128)(2,1)S(1)} %all-to-all-done.1.bias_ref), channel_id=1, source_target_pairs={{0,16},{16,0},{1,17},{17,1},{2,18},{18,2},{3,19},{19,3},{4,20},{20... | collective-permute-start | bytes 3538952 | tf_op jit(solution)/shard_map/ppermute | solution.py:191
  75.6 0.8 copy-start.3

commit v3 on v2

--- a/solution.py
+++ b/solution.py
@@ -84,7 +84,7 @@
             jax.ShapeDtypeStruct((2, rows, count // 4, width), jnp.float32),
         ),
         compiler_params=pltpu.CompilerParams(vmem_limit_bytes=16 * 2**20),
-        cost_estimate=pl.CostEstimate(flops=10**9, bytes_accessed=10**7, transcendentals=10**6),
+        cost_estimate=pl.CostEstimate(flops=2 * 10**10, bytes_accessed=10**7, transcendentals=10**6),
         name="project",
     )(own, far, wq, wk, wvt, wg)
 
@@ -187,7 +187,7 @@
     bias, near = lax.optimization_barrier((bias, got[:, :-1]))
     far = lax.ppermute(near, "zh", flip)
     bias = gather(bias, ("zl0", "x"))
-    bias, far = lax.optimization_barrier((bias, far))
+
     other = lax.ppermute(bias, "core", flip)
     penalty = jnp.where(valid == 1, 0.0, -1000000000.0).astype(jnp.float32).reshape(2, -1)
     penalty = jnp.where(first_z, penalty, penalty[::-1]).reshape(-1, 1)

time: 102 us -> 97.2 us (0.953)
  waiting for transfers between devices: 26.3 us -> 23.8 us
  blocking collectives: 38.8 us -> 36.5 us
    ppermute x1, waiting for transfers between devices: 21.6 us -> 3.1 us  [local(): far = lax.ppermute(near, 'zh', flip)]
    all_to_all x1, waiting for transfers between devices: 0.01 us -> 16 us  [gather(): lax.all_to_all(jnp.broadcast_to(block[None], (size,) + block.shape), axes...]
    all_to_all x1, blocking collectives: 17.1 us -> 14.7 us  [local(): lax.all_to_all(update, 'y', 0, 0, tiled=True).reshape(rows, cols, width)]
  transfers between devices with their start and end apart: 5 -> 5, of which waited for: 3 -> 4; matrix products, arithmetic and copies ran while one was open for 0% -> 0% of each run, Pallas kernels for 4% -> 4%
where the time goes in v3:
time: 97.2 us; the launch traced here: 96.7 us
  blocking collectives  36.5 us (38%)
  waiting for transfers between devices  23.8 us (24%)
  starting transfers between devices  23 us (24%)
  Pallas kernels  10.6 us (11%)
  local copies, waits for them, and re-layouts  2.48 us (3%)
    all_to_all x1, blocking collectives, local(): lax.all_to_all(normalize(pair, ln_gain.reshape(1, width), w_bias.T, ring)...  21.8 us
    all_to_all x1, waiting for transfers between devices, gather(): lax.all_to_all(jnp.broadcast_to(block[None], (size,) + block.shape), axes...  16 us
    all_to_all x1, blocking collectives, local(): lax.all_to_all(update, 'y', 0, 0, tiled=True).reshape(rows, cols, width)  14.7 us
    pallas_call x2, Pallas kernels, attend(): pl.pallas_call(functools.partial(attend_kernel, before is None), out_shap...  7.3 us
    ppermute x1, starting transfers between devices, local(): same = lax.ppermute(bias, ('zl1', 'zh'), [(0, 0), (1, 2), (2, 1), (3, 3)])  7.3 us
    all_to_all x1, starting transfers between devices, gather(): lax.all_to_all(jnp.broadcast_to(block[None], (size,) + block.shape), axes...  6.58 us
    ppermute x1, starting transfers between devices, local(): far = lax.ppermute(near, 'zh', flip)  4.7 us
    ppermute x1, waiting for transfers between devices, local(): swap = lax.ppermute(bias, ('zl1', 'zh'), [(0, 2), (1, 0), (2, 3), (3, 1)])  3.59 us
  transfers between devices with their start and end apart: 5, of which 4 were waited for; matrix products, arithmetic and copies ran while one was open for 0% of the time, Pallas kernels for 4%

profile of v3, /device:TPU:130, one launch (start us, length us, event | category | flops | bytes accessed | tf_op | source)
XLA Modules:
  0.0 96.7 jit_solution(4259434718198211063)
XLA Ops:
  0.0 2.6 %normalize.1 = bf16[8,4,48,128]{3,2,1,0:T(8,128)(2,1)} custom-call(bf16[24,48,128]{2,1,0:T(8,128)(2,1)} %pair_ref.1, f32[1,128]{1,0:T(1,128)} %bitcast.30, bf16[4,128]{1,0:T(4,128)(2,1)} %bitcast.29), custom_call_target="tpu_custom_call" | custom-call | tf_op jit(solution)/shard_map/normalize/pallas_call | solution.py:46
  2.6 21.8 %all_to_all.15 = bf16[8,4,48,128]{3,2,1,0:T(8,128)(2,1)S(1)} all-to-all(bf16[8,4,48,128]{3,2,1,0:T(8,128)(2,1)} %normalize.1), channel_id=1, replica_groups=mesh['zl1'=2,'zl0'=2,'x'=4,'core'=2,'zh'=2,'y'=8] {'y'}, dimensions={0} | all-to-all | bytes 786432 | tf_op jit(solution)/shard_map/all_to_all | solution.py:180
  24.5 0.1 pad_maximum_fusion.1
  24.6 7.3 %collective-permute-start = (bf16[96,384]{1,0:T(8,128)(2,1)S(1)}, bf16[96,384]{1,0:T(8,128)(2,1)S(1)}, u32[]{:S(2)}, u32[]{:S(2)}) collective-permute-start(bf16[96,384]{1,0:T(8,128)(2,1)S(1)} %pad_maximum_fusion.1), channel_id=1, source_target_pairs={{0,0},{8,256},{256,8},{264,264},{1,1},{9,257},{257,9},{265,265},{2... | collective-permute-start | bytes 221192 | tf_op jit(solution)/shard_map/ppermute | solution.py:183
  31.9 2.5 %collective-permute-start.1 = (bf16[96,384]{1,0:T(8,128)(2,1)S(1)}, bf16[96,384]{1,0:T(8,128)(2,1)S(1)}, u32[]{:S(2)}, u32[]{:S(2)}) collective-permute-start(bf16[96,384]{1,0:T(8,128)(2,1)S(1)} %pad_maximum_fusion.1), channel_id=1, source_target_pairs={{0,256},{8,0},{256,264},{264,8},{1,257},{9,1},{257,265},{265,9},{2... | collective-permute-start | bytes 221192 | tf_op jit(solution)/shard_map/ppermute | solution.py:184
  34.4 1.1 %collective-permute-done = bf16[96,384]{1,0:T(8,128)(2,1)S(1)} collective-permute-done((bf16[96,384]{1,0:T(8,128)(2,1)S(1)}, bf16[96,384]{1,0:T(8,128)(2,1)S(1)}, u32[]{:S(2)}, u32[]{:S(2)}) %collective-permute-start) | collective-permute-done | bytes 73760 | tf_op jit(solution)/shard_map/ppermute | solution.py:183
  35.5 3.6 %collective-permute-done.1 = bf16[96,384]{1,0:T(8,128)(2,1)S(1)} collective-permute-done((bf16[96,384]{1,0:T(8,128)(2,1)S(1)}, bf16[96,384]{1,0:T(8,128)(2,1)S(1)}, u32[]{:S(2)}, u32[]{:S(2)}) %collective-permute-start.1) | collective-permute-done | bytes 73760 | tf_op jit(solution)/shard_map/ppermute | solution.py:184
  39.2 1.2 %broadcast_in_dim.14 = bf16[8,2,96,384]{3,2,1,0:T(8,128)(2,1)} broadcast(bf16[2,96,384]{2,1,0:T(8,128)(2,1)S(1)} %pad_maximum_fusion), dimensions={1,2,3} | broadcast | bytes 1327104 | tf_op jit(solution)/shard_map/broadcast_in_dim | solution.py:171
  40.3 0.0 copy-start.5
  40.3 0.0 copy-start.4
  40.3 0.0 copy-start.2
  40.4 6.6 %all-to-all-start.1 = ((bf16[8,2,96,384]{3,2,1,0:T(8,128)(2,1)}), bf16[8,2,96,384]{3,2,1,0:T(8,128)(2,1)S(1)}, u32[]{:S(2)}, u32[]{:S(2)}) async-start(bf16[8,2,96,384]{3,2,1,0:T(8,128)(2,1)} %broadcast_in_dim.14), calls=%async_computation.1 | async-start | bytes 2359296 | tf_op jit(solution)/shard_map/all_to_all | solution.py:171
  46.9 4.7 %collective-permute-start.3 = (bf16[8,3,48,128]{3,2,1,0:T(8,128)(2,1)S(1)}, bf16[8,3,48,128]{3,2,1,0:T(8,128)(2,1)S(1)}, u32[]{:S(2)}, u32[]{:S(2)}) collective-permute-start(bf16[8,3,48,128]{3,2,1,0:T(8,128)(2,1)S(1)} %slice.29.own_ref), channel_id=1, source_target_pairs={{0,8},{8,0},{1,9},{9,1},{2,10},{10,2},{3,11},{11,3},{4,12},{12,4},... | collective-permute-start | bytes 884744 | tf_op jit(solution)/shard_map/ppermute | solution.py:188
  51.6 0.0 copy-done.5
  51.7 0.0 copy-done.4
  51.7 0.1 copy.11
  51.8 0.1 rev.3
  51.9 0.2 copy.15
  52.1 16.0 %all-to-all-done.1.bias_ref = bf16[8,2,96,384]{3,2,1,0:T(8,128)(2,1)S(1)} async-done(((bf16[8,2,96,384]{3,2,1,0:T(8,128)(2,1)}), bf16[8,2,96,384]{3,2,1,0:T(8,128)(2,1)S(1)}, u32[]{:S(2)}, u32[]{:S(2)}) %all-to-all-start.1) | async-done | bytes 1179680 | tf_op jit(solution)/shard_map/all_to_all | solution.py:171
  68.2 1.9 %collective-permute-start.2 = (bf16[8,2,96,384]{3,2,1,0:T(8,128)(2,1)S(1)}, bf16[8,2,96,384]{3,2,1,0:T(8,128)(2,1)S(1)}, u32[]{:S(2)}, u32[]{:S(2)}) collective-permute-start(bf16[8,2,96,384]{3,2,1,0:T(8,128)(2,1)S(1)} %all-to-all-done.1.bias_ref), channel_id=1, source_target_pairs={{0,16},{16,0},{1,17},{17,1},{2,18},{18,2},{3,19},{19,3},{4,20},{20... | collective-permute-start | bytes 3538952 | tf_op jit(solution)/shard_map/ppermute | solution.py:191
  70.1 3.1 %collective-permute-done.3.far_ref = bf16[8,3,48,128]{3,2,1,0:T(8,128)(2,1)S(1)} collective-permute-done((bf16[8,3,48,128]{3,2,1,0:T(8,128)(2,1)S(1)}, bf16[8,3,48,128]{3,2,1,0:T(8,128)(2,1)S(1)}, u32[]{:S(2)}, u32[]{:S(2)}) %collective-permute-start.3) | collective-permute-done | bytes 294944 | tf_op jit(solution)/shard_map/ppermute | solution.py:188
  73.2 0.0 copy-done
  73.2 0.0 copy-done.1
  73.2 0.0 copy-done.2
  73.2 0.0 copy-start.3
  73.2 0.6 project.1
  73.8 0.1 copy-done.3
  74.0 3.6 %attend.2.refs_0_ = f32[8,3,24,128]{3,2,1,0:T(8,128)S(1)} custom-call(s32[1]{0:T(128)} %bitcast.half_ref, bf16[8,2,96,384]{3,2,1,0:T(8,128)(2,1)S(1)} %all-to-all-done.1.bias_ref, f32[768,1]{1,0:T(8,128)S(1)} %bitcast.23, bf16[3,768,128]{2,1,0:T(8,128)(2,1)S(1)} %get-tuple-element.13.key_ref, bf16[3,128,768]{2,1,0:T(8,128)(2,1)S(1)} %get-tuple-element.14.value_ref, ...), custom_call_target="tpu_custom_call" | custom-call | flops 2000000000 | bytes 20000000 | tf_op jit(solution)/shard_map/attend/pallas_call | solution.py:157
  77.6 0.0 collective-permute-done.2.bias_ref
  77.6 3.7 %attend.3 = bf16[8,3,48,128]{3,2,1,0:T(8,128)(2,1)S(1)} custom-call(s32[1]{0:T(128)S(6)} %sub.3.half_ref, bf16[8,2,96,384]{3,2,1,0:T(8,128)(2,1)S(1)} %collective-permute-done.2.bias_ref, f32[768,1]{1,0:T(8,128)S(1)} %bitcast.24, bf16[3,768,128]{2,1,0:T(8,128)(2,1)S(1)} %get-tuple-element.13.key_ref, bf16[3,128,768]{2,1,0:T(8,128)(2,1)S(1)} %get-tuple-element.14.value_ref, ...), custom_call_target="tpu_custom_call" | custom-call | flops 2000000000 | bytes 20000000 | tf_op jit(solution)/shard_map/attend/pallas_call | solution.py:157
  81.3 14.7 %all_to_all.16 = bf16[8,3,48,128]{3,2,1,0:T(8,128)(2,1)S(1)} all-to-all(bf16[8,3,48,128]{3,2,1,0:T(8,128)(2,1)S(1)} %attend.3), channel_id=1, replica_groups=mesh['zl1'=2,'zl0'=2,'x'=4,'core'=2,'zh'=2,'y'=8] {'y'}, dimensions={0} | all-to-all | bytes 589824 | tf_op jit(solution)/shard_map/all_to_all | solution.py:197
  96.0 0.7 copy.17
  (11 shorter events, 0.1 us)
Async XLA Ops:
  24.6 10.9 %collective-permute-start = (bf16[96,384]{1,0:T(8,128)(2,1)S(1)}, bf16[96,384]{1,0:T(8,128)(2,1)S(1)}, u32[]{:S(2)}, u32[]{:S(2)}) collective-permute-start(bf16[96,384]{1,0:T(8,128)(2,1)S(1)} %pad_maximum_fusion.1), channel_id=1, source_target_pairs={{0,0},{8,256},{256,8},{264,264},{1,1},{9,257},{257,9},{265,265},{2... | collective-permute-start | bytes 221192 | tf_op jit(solution)/shard_map/ppermute | solution.py:183
  31.9 7.2 %collective-permute-start.1 = (bf16[96,384]{1,0:T(8,128)(2,1)S(1)}, bf16[96,384]{1,0:T(8,128)(2,1)S(1)}, u32[]{:S(2)}, u32[]{:S(2)}) collective-permute-start(bf16[96,384]{1,0:T(8,128)(2,1)S(1)} %pad_maximum_fusion.1), channel_id=1, source_target_pairs={{0,256},{8,0},{256,264},{264,8},{1,257},{9,1},{257,265},{265,9},{2... | collective-permute-start | bytes 221192 | tf_op jit(solution)/shard_map/ppermute | solution.py:184
  40.3 11.3 %copy-start.5 = (s32[768]{0:T(1024)S(1)}, s32[768]{0:T(1024)}, u32[]{:S(2)}) copy-start(s32[768]{0:T(1024)} %param.10) | copy-start | bytes 9220
  40.3 11.3 %copy-start.4 = (bf16[128,128]{1,0:T(8,128)(2,1)S(1)}, bf16[128,128]{1,0:T(8,128)(2,1)}, u32[]{:S(2)}) copy-start(bf16[128,128]{1,0:T(8,128)(2,1)} %param.14) | copy-start | bytes 98308
  40.3 32.9 %copy-start = (bf16[128,128]{1,0:T(8,128)(2,1)S(1)}, bf16[128,128]{1,0:T(8,128)(2,1)}, u32[]{:S(2)}) copy-start(bf16[128,128]{1,0:T(8,128)(2,1)} %wq_ref.1) | copy-start | bytes 98308
  40.3 32.9 %copy-start.1 = (bf16[128,128]{1,0:T(8,128)(2,1)S(1)}, bf16[128,128]{1,0:T(8,128)(2,1)}, u32[]{:S(2)}) copy-start(bf16[128,128]{1,0:T(8,128)(2,1)} %wk_ref.1) | copy-start | bytes 98308
  40.3 32.9 %copy-start.2 = (bf16[128,128]{1,0:T(8,128)(2,1)S(1)}, bf16[128,128]{1,0:T(8,128)(2,1)}, u32[]{:S(2)}) copy-start(bf16[128,128]{1,0:T(8,128)(2,1)} %wg_ref.1) | copy-start | bytes 98308
  40.4 27.8 %all-to-all-start.1 = ((bf16[8,2,96,384]{3,2,1,0:T(8,128)(2,1)}), bf16[8,2,96,384]{3,2,1,0:T(8,128)(2,1)S(1)}, u32[]{:S(2)}, u32[]{:S(2)}) async-start(bf16[8,2,96,384]{3,2,1,0:T(8,128)(2,1)} %broadcast_in_dim.14), calls=%async_computation.1 | async-start | bytes 2359296 | tf_op jit(solution)/shard_map/all_to_all | solution.py:171
  46.9 26.3 %collective-permute-start.3 = (bf16[8,3,48,128]{3,2,1,0:T(8,128)(2,1)S(1)}, bf16[8,3,48,128]{3,2,1,0:T(8,128)(2,1)S(1)}, u32[]{:S(2)}, u32[]{:S(2)}) collective-permute-start(bf16[8,3,48,128]{3,2,1,0:T(8,128)(2,1)S(1)} %slice.29.own_ref), channel_id=1, source_target_pairs={{0,8},{8,0},{1,9},{9,1},{2,10},{10,2},{3,11},{11,3},{4,12},{12,4},... | collective-permute-start | bytes 884744 | tf_op jit(solution)/shard_map/ppermute | solution.py:188
  68.2 9.4 %collective-permute-start.2 = (bf16[8,2,96,384]{3,2,1,0:T(8,128)(2,1)S(1)}, bf16[8,2,96,384]{3,2,1,0:T(8,128)(2,1)S(1)}, u32[]{:S(2)}, u32[]{:S(2)}) collective-permute-start(bf16[8,2,96,384]{3,2,1,0:T(8,128)(2,1)S(1)} %all-to-all-done.1.bias_ref), channel_id=1, source_target_pairs={{0,16},{16,0},{1,17},{17,1},{2,18},{18,2},{3,19},{19,3},{4,20},{20... | collective-permute-start | bytes 3538952 | tf_op jit(solution)/shard_map/ppermute | solution.py:191
  73.2 0.8 copy-start.3

commit v4 on v3

--- a/solution.py
+++ b/solution.py
@@ -98,7 +98,7 @@
     lanes = query_ref.shape[2] // blocks
     step = lanes // HEADS
     here = blocks * step
-    quarter = bias_ref.shape[2]
+    xs, quarter = bias_ref.shape[0], bias_ref.shape[3]
     part, chunk = 48, 128
     half = half_ref[0]
     masks = [head_mask(step, h) for h in range(HEADS)]
@@ -106,7 +106,8 @@
     for k in range(0, count, part):
         z, m, at = k // (HEADS * quarter), k // quarter % HEADS, k % quarter
         pieces = [
-            bias_ref[b, z, at : at + part, m * lanes : (m + 1) * lanes].astype(jnp.float32) for b in range(blocks)
+            bias_ref[b % xs, b // xs, z, at : at + part, m * lanes : (m + 1) * lanes].astype(jnp.float32)
+            for b in range(blocks)
         ]
         score_bias[k : k + part, :] = jnp.concatenate(pieces, axis=1) + pen_ref[k : k + part, :]
 
@@ -144,7 +145,7 @@
 
 
 def attend(half, bias, penalty, keys, values, query, gate, wo, before=None):
-    blocks = bias.shape[0]
+    blocks = bias.shape[0] * bias.shape[1]
     rows, count, width = keys.shape
     here = query.shape[2]
     step = here // HEADS // blocks
@@ -180,14 +181,16 @@
     got = lax.all_to_all(normalize(pair, ln_gain.reshape(1, width), w_bias.T, ring), "y", 0, 0, tiled=True)
     bias = got[:, -1].reshape(HEADS, -1, 128)
     bias = jnp.concatenate([bias[m, :, : rows * HEADS] for m in range(HEADS)], axis=1)
+    low = lax.axis_index("zl0") == 0
+    straight = lax.axis_index("zl1") == lax.axis_index("zh")
+    beside = lax.ppermute(bias, "zl0", flip)
+    bias = jnp.stack([jnp.where(low, bias, beside), jnp.where(low, beside, bias)])
     same = lax.ppermute(bias, ("zl1", "zh"), [(0, 0), (1, 2), (2, 1), (3, 3)])
     swap = lax.ppermute(bias, ("zl1", "zh"), [(0, 2), (1, 0), (2, 3), (3, 1)])
-    straight = lax.axis_index("zl1") == lax.axis_index("zh")
-    bias = jnp.stack([jnp.where(straight, same, swap), jnp.where(straight, swap, same)])
+    bias = jnp.stack([jnp.where(straight, same, swap), jnp.where(straight, swap, same)], axis=1)
     bias, near = lax.optimization_barrier((bias, got[:, :-1]))
     far = lax.ppermute(near, "zh", flip)
-    bias = gather(bias, ("zl0", "x"))
-
+    bias = gather(bias, "x")
     other = lax.ppermute(bias, "core", flip)
     penalty = jnp.where(valid == 1, 0.0, -1000000000.0).astype(jnp.float32).reshape(2, -1)
     penalty = jnp.where(first_z, penalty, penalty[::-1]).reshape(-1, 1)

time: 97.2 us -> 96.5 us (level)
  the two profiles are of different devices: /device:TPU:130 before, /device:TPU:2 now
where the time goes in v4:
time: 96.5 us; the launch traced here: 95.9 us
  blocking collectives  35 us (36%)
  starting transfers between devices  28.5 us (30%)
  waiting for transfers between devices  18.9 us (20%)
  Pallas kernels  10.6 us (11%)
  local copies, waits for them, and re-layouts  2.47 us (3%)
    all_to_all x1, blocking collectives, local(): lax.all_to_all(normalize(pair, ln_gain.reshape(1, width), w_bias.T, ring)...  21.8 us
    all_to_all x1, blocking collectives, local(): lax.all_to_all(update, 'y', 0, 0, tiled=True).reshape(rows, cols, width)  13.2 us
    ppermute x1, starting transfers between devices, local(): swap = lax.ppermute(bias, ('zl1', 'zh'), [(0, 2), (1, 0), (2, 3), (3, 1)])  12.4 us
    pallas_call x2, Pallas kernels, attend(): pl.pallas_call(functools.partial(attend_kernel, before is None), out_shap...  7.31 us
    ppermute x1, waiting for transfers between devices, local(): far = lax.ppermute(near, 'zh', flip)  6.64 us
    all_to_all x1, waiting for transfers between devices, gather(): lax.all_to_all(jnp.broadcast_to(block[None], (size,) + block.shape), axes...  5.32 us
    all_to_all x1, starting transfers between devices, gather(): lax.all_to_all(jnp.broadcast_to(block[None], (size,) + block.shape), axes...  4.96 us
    ppermute x1, waiting for transfers between devices, local(): swap = lax.ppermute(bias, ('zl1', 'zh'), [(0, 2), (1, 0), (2, 3), (3, 1)])  4.6 us
  transfers between devices with their start and end apart: 6, of which 4 were waited for; matrix products, arithmetic and copies ran while one was open for 0% of the time, Pallas kernels for 4%

profile of v4, /device:TPU:2, one launch (start us, length us, event | category | flops | bytes accessed | tf_op | source)
XLA Modules:
  0.0 95.9 jit_solution(15274001156765841522)
XLA Ops:
  0.0 2.7 %normalize.1 = bf16[8,4,48,128]{3,2,1,0:T(8,128)(2,1)} custom-call(bf16[24,48,128]{2,1,0:T(8,128)(2,1)} %pair_ref.1, f32[1,128]{1,0:T(1,128)} %bitcast.36, bf16[4,128]{1,0:T(4,128)(2,1)} %bitcast.35), custom_call_target="tpu_custom_call" | custom-call | tf_op jit(solution)/shard_map/normalize/pallas_call | solution.py:46
  2.7 21.8 %all_to_all.15 = bf16[8,4,48,128]{3,2,1,0:T(8,128)(2,1)S(1)} all-to-all(bf16[8,4,48,128]{3,2,1,0:T(8,128)(2,1)} %normalize.1), channel_id=1, replica_groups=mesh['zl1'=2,'zl0'=2,'x'=4,'core'=2,'zh'=2,'y'=8] {'y'}, dimensions={0} | all-to-all | bytes 786432 | tf_op jit(solution)/shard_map/all_to_all | solution.py:181
  24.5 0.1 pad_maximum_fusion.2
  24.6 4.3 %collective-permute-start = (bf16[96,384]{1,0:T(8,128)(2,1)S(1)}, bf16[96,384]{1,0:T(8,128)(2,1)S(1)}, u32[]{:S(2)}, u32[]{:S(2)}) collective-permute-start(bf16[96,384]{1,0:T(8,128)(2,1)S(1)} %pad_maximum_fusion.2), channel_id=1, source_target_pairs={{0,128},{128,0},{1,129},{129,1},{2,130},{130,2},{3,131},{131,3},{4... | collective-permute-start | bytes 221192 | tf_op jit(solution)/shard_map/ppermute | solution.py:186
  28.9 2.3 %collective-permute-done = bf16[96,384]{1,0:T(8,128)(2,1)S(1)} collective-permute-done((bf16[96,384]{1,0:T(8,128)(2,1)S(1)}, bf16[96,384]{1,0:T(8,128)(2,1)S(1)}, u32[]{:S(2)}, u32[]{:S(2)}) %collective-permute-start) | collective-permute-done | bytes 73760 | tf_op jit(solution)/shard_map/ppermute | solution.py:186
  31.2 0.1 select_bitcast_fusion.3
  31.3 0.7 collective-permute-start.1
  32.0 12.4 %collective-permute-start.2 = (bf16[2,96,384]{2,1,0:T(8,128)(2,1)S(1)}, bf16[2,96,384]{2,1,0:T(8,128)(2,1)S(1)}, u32[]{:S(2)}, u32[]{:S(2)}) collective-permute-start(bf16[2,96,384]{2,1,0:T(8,128)(2,1)S(1)} %pad_maximum_fusion.1), channel_id=1, source_target_pairs={{0,256},{8,0},{256,264},{264,8},{1,257},{9,1},{257,265},{265,9},{2... | collective-permute-start | bytes 442376 | tf_op jit(solution)/shard_map/ppermute | solution.py:189
  44.4 0.0 collective-permute-done.1
  44.4 4.6 %collective-permute-done.2 = bf16[2,96,384]{2,1,0:T(8,128)(2,1)S(1)} collective-permute-done((bf16[2,96,384]{2,1,0:T(8,128)(2,1)S(1)}, bf16[2,96,384]{2,1,0:T(8,128)(2,1)S(1)}, u32[]{:S(2)}, u32[]{:S(2)}) %collective-permute-start.2) | collective-permute-done | bytes 147488 | tf_op jit(solution)/shard_map/ppermute | solution.py:189
  49.1 1.2 %broadcast_in_dim.14 = bf16[4,2,2,96,384]{4,3,2,1,0:T(8,128)(2,1)} broadcast(bf16[2,2,96,384]{3,2,1,0:T(8,128)(2,1)S(1)} %pad_maximum_fusion), dimensions={1,2,3,4} | broadcast | bytes 1474560 | tf_op jit(solution)/shard_map/broadcast_in_dim | solution.py:172
  50.3 0.0 copy-start.2
  50.3 5.0 %all-to-all-start.1 = ((bf16[4,2,2,96,384]{4,3,2,1,0:T(8,128)(2,1)}), bf16[4,2,2,96,384]{4,3,2,1,0:T(8,128)(2,1)S(1)}, u32[]{:S(2)}, u32[]{:S(2)}) async-start(bf16[4,2,2,96,384]{4,3,2,1,0:T(8,128)(2,1)} %broadcast_in_dim.14), calls=%async_computation.1 | async-start | bytes 2359296 | tf_op jit(solution)/shard_map/all_to_all | solution.py:172
  55.3 4.3 %collective-permute-start.4 = (bf16[8,3,48,128]{3,2,1,0:T(8,128)(2,1)S(1)}, bf16[8,3,48,128]{3,2,1,0:T(8,128)(2,1)S(1)}, u32[]{:S(2)}, u32[]{:S(2)}) collective-permute-start(bf16[8,3,48,128]{3,2,1,0:T(8,128)(2,1)S(1)} %slice.29.own_ref), channel_id=1, source_target_pairs={{0,8},{8,0},{1,9},{9,1},{2,10},{10,2},{3,11},{11,3},{4,12},{12,4},... | collective-permute-start | bytes 884744 | tf_op jit(solution)/shard_map/ppermute | solution.py:192
  59.6 0.0 copy-done.5
  59.6 0.0 copy-done.4
  59.6 0.1 copy.13
  59.7 0.1 rev.3
  59.9 0.2 copy.17
  60.1 5.3 %all-to-all-done.1.bias_ref = bf16[4,2,2,96,384]{4,3,2,1,0:T(8,128)(2,1)S(1)} async-done(((bf16[4,2,2,96,384]{4,3,2,1,0:T(8,128)(2,1)}), bf16[4,2,2,96,384]{4,3,2,1,0:T(8,128)(2,1)S(1)}, u32[]{:S(2)}, u32[]{:S(2)}) %all-to-all-start.1) | async-done | bytes 1179680 | tf_op jit(solution)/shard_map/all_to_all | solution.py:172
  65.4 1.9 %collective-permute-start.3 = (bf16[4,2,2,96,384]{4,3,2,1,0:T(8,128)(2,1)S(1)}, bf16[4,2,2,96,384]{4,3,2,1,0:T(8,128)(2,1)S(1)}, u32[]{:S(2)}, u32[]{:S(2)}) collective-permute-start(bf16[4,2,2,96,384]{4,3,2,1,0:T(8,128)(2,1)S(1)} %all-to-all-done.1.bias_ref), channel_id=1, source_target_pairs={{0,16},{16,0},{1,17},{17,1},{2,18},{18,2},{3,19},{19,3},{4,20},{20... | collective-permute-start | bytes 3538952 | tf_op jit(solution)/shard_map/ppermute | solution.py:194
  67.3 6.6 %collective-permute-done.4.far_ref = bf16[8,3,48,128]{3,2,1,0:T(8,128)(2,1)S(1)} collective-permute-done((bf16[8,3,48,128]{3,2,1,0:T(8,128)(2,1)S(1)}, bf16[8,3,48,128]{3,2,1,0:T(8,128)(2,1)S(1)}, u32[]{:S(2)}, u32[]{:S(2)}) %collective-permute-start.4) | collective-permute-done | bytes 294944 | tf_op jit(solution)/shard_map/ppermute | solution.py:192
  74.0 0.0 copy-done
  74.0 0.0 copy-done.1
  74.0 0.0 copy-start.3
  74.0 0.6 project.1
  74.6 0.1 copy-done.3
  74.7 3.6 %attend.2.refs_0_ = f32[8,3,24,128]{3,2,1,0:T(8,128)S(1)} custom-call(s32[1]{0:T(128)} %bitcast.half_ref, bf16[4,2,2,96,384]{4,3,2,1,0:T(8,128)(2,1)S(1)} %all-to-all-done.1.bias_ref, f32[768,1]{1,0:T(8,128)S(1)} %bitcast.29, bf16[3,768,128]{2,1,0:T(8,128)(2,1)S(1)} %get-tuple-element.13.key_ref, bf16[3,128,768]{2,1,0:T(8,128)(2,1)S(1)} %get-tuple-element.14.value_ref, ...), custom_call_target="tpu_custom_call" | custom-call | flops 2000000000 | bytes 20000000 | tf_op jit(solution)/shard_map/attend/pallas_call | solution.py:158
  78.4 0.0 collective-permute-done.3.bias_ref
  78.4 3.7 %attend.3 = bf16[8,3,48,128]{3,2,1,0:T(8,128)(2,1)S(1)} custom-call(s32[1]{0:T(128)S(6)} %sub.3.half_ref, bf16[4,2,2,96,384]{4,3,2,1,0:T(8,128)(2,1)S(1)} %collective-permute-done.3.bias_ref, f32[768,1]{1,0:T(8,128)S(1)} %bitcast.30, bf16[3,768,128]{2,1,0:T(8,128)(2,1)S(1)} %get-tuple-element.13.key_ref, ...), custom_call_target="tpu_custom_call" | custom-call | flops 2000000000 | bytes 20000000 | tf_op jit(solution)/shard_map/attend/pallas_call | solution.py:158
  82.0 13.2 %all_to_all.16 = bf16[8,3,48,128]{3,2,1,0:T(8,128)(2,1)S(1)} all-to-all(bf16[8,3,48,128]{3,2,1,0:T(8,128)(2,1)S(1)} %attend.3), channel_id=1, replica_groups=mesh['zl1'=2,'zl0'=2,'x'=4,'core'=2,'zh'=2,'y'=8] {'y'}, dimensions={0} | all-to-all | bytes 589824 | tf_op jit(solution)/shard_map/all_to_all | solution.py:200
  95.2 0.7 copy.19
  (15 shorter events, 0.2 us)
Async XLA Ops:
  24.6 6.6 %collective-permute-start = (bf16[96,384]{1,0:T(8,128)(2,1)S(1)}, bf16[96,384]{1,0:T(8,128)(2,1)S(1)}, u32[]{:S(2)}, u32[]{:S(2)}) collective-permute-start(bf16[96,384]{1,0:T(8,128)(2,1)S(1)} %pad_maximum_fusion.2), channel_id=1, source_target_pairs={{0,128},{128,0},{1,129},{129,1},{2,130},{130,2},{3,131},{131,3},{4... | collective-permute-start | bytes 221192 | tf_op jit(solution)/shard_map/ppermute | solution.py:186
  31.3 13.1 %collective-permute-start.1 = (bf16[2,96,384]{2,1,0:T(8,128)(2,1)S(1)}, bf16[2,96,384]{2,1,0:T(8,128)(2,1)S(1)}, u32[]{:S(2)}, u32[]{:S(2)}) collective-permute-start(bf16[2,96,384]{2,1,0:T(8,128)(2,1)S(1)} %pad_maximum_fusion.1), channel_id=1, source_target_pairs={{0,0},{8,256},{256,8},{264,264},{1,1},{9,257},{257,9},{265,265},{2... | collective-permute-start | bytes 442376 | tf_op jit(solution)/shard_map/ppermute | solution.py:188
  32.0 17.0 %collective-permute-start.2 = (bf16[2,96,384]{2,1,0:T(8,128)(2,1)S(1)}, bf16[2,96,384]{2,1,0:T(8,128)(2,1)S(1)}, u32[]{:S(2)}, u32[]{:S(2)}) collective-permute-start(bf16[2,96,384]{2,1,0:T(8,128)(2,1)S(1)} %pad_maximum_fusion.1), channel_id=1, source_target_pairs={{0,256},{8,0},{256,264},{264,8},{1,257},{9,1},{257,265},{265,9},{2... | collective-permute-start | bytes 442376 | tf_op jit(solution)/shard_map/ppermute | solution.py:189
  50.3 9.3 %copy-start.5 = (s32[768]{0:T(1024)S(1)}, s32[768]{0:T(1024)}, u32[]{:S(2)}) copy-start(s32[768]{0:T(1024)} %param.10) | copy-start | bytes 9220
  50.3 9.3 %copy-start.4 = (bf16[128,128]{1,0:T(8,128)(2,1)S(1)}, bf16[128,128]{1,0:T(8,128)(2,1)}, u32[]{:S(2)}) copy-start(bf16[128,128]{1,0:T(8,128)(2,1)} %param.14) | copy-start | bytes 98308
  50.3 23.7 %copy-start = (bf16[128,128]{1,0:T(8,128)(2,1)S(1)}, bf16[128,128]{1,0:T(8,128)(2,1)}, u32[]{:S(2)}) copy-start(bf16[128,128]{1,0:T(8,128)(2,1)} %wq_ref.1) | copy-start | bytes 98308
  50.3 23.7 %copy-start.1 = (bf16[128,128]{1,0:T(8,128)(2,1)S(1)}, bf16[128,128]{1,0:T(8,128)(2,1)}, u32[]{:S(2)}) copy-start(bf16[128,128]{1,0:T(8,128)(2,1)} %wk_ref.1) | copy-start | bytes 98308
  50.3 23.7 %copy-start.2 = (bf16[128,128]{1,0:T(8,128)(2,1)S(1)}, bf16[128,128]{1,0:T(8,128)(2,1)}, u32[]{:S(2)}) copy-start(bf16[128,128]{1,0:T(8,128)(2,1)} %wg_ref.1) | copy-start | bytes 98308
  50.3 15.1 %all-to-all-start.1 = ((bf16[4,2,2,96,384]{4,3,2,1,0:T(8,128)(2,1)}), bf16[4,2,2,96,384]{4,3,2,1,0:T(8,128)(2,1)S(1)}, u32[]{:S(2)}, u32[]{:S(2)}) async-start(bf16[4,2,2,96,384]{4,3,2,1,0:T(8,128)(2,1)} %broadcast_in_dim.14), calls=%async_computation.1 | async-start | bytes 2359296 | tf_op jit(solution)/shard_map/all_to_all | solution.py:172
  55.3 18.7 %collective-permute-start.4 = (bf16[8,3,48,128]{3,2,1,0:T(8,128)(2,1)S(1)}, bf16[8,3,48,128]{3,2,1,0:T(8,128)(2,1)S(1)}, u32[]{:S(2)}, u32[]{:S(2)}) collective-permute-start(bf16[8,3,48,128]{3,2,1,0:T(8,128)(2,1)S(1)} %slice.29.own_ref), channel_id=1, source_target_pairs={{0,8},{8,0},{1,9},{9,1},{2,10},{10,2},{3,11},{11,3},{4,12},{12,4},... | collective-permute-start | bytes 884744 | tf_op jit(solution)/shard_map/ppermute | solution.py:192
  65.4 13.0 %collective-permute-start.3 = (bf16[4,2,2,96,384]{4,3,2,1,0:T(8,128)(2,1)S(1)}, bf16[4,2,2,96,384]{4,3,2,1,0:T(8,128)(2,1)S(1)}, u32[]{:S(2)}, u32[]{:S(2)}) collective-permute-start(bf16[4,2,2,96,384]{4,3,2,1,0:T(8,128)(2,1)S(1)} %all-to-all-done.1.bias_ref), channel_id=1, source_target_pairs={{0,16},{16,0},{1,17},{17,1},{2,18},{18,2},{3,19},{19,3},{4,20},{20... | collective-permute-start | bytes 3538952 | tf_op jit(solution)/shard_map/ppermute | solution.py:194
  74.0 0.8 copy-start.3

commit v5 on v4

--- a/solution.py
+++ b/solution.py
@@ -188,7 +188,7 @@
     same = lax.ppermute(bias, ("zl1", "zh"), [(0, 0), (1, 2), (2, 1), (3, 3)])
     swap = lax.ppermute(bias, ("zl1", "zh"), [(0, 2), (1, 0), (2, 3), (3, 1)])
     bias = jnp.stack([jnp.where(straight, same, swap), jnp.where(straight, swap, same)], axis=1)
-    bias, near = lax.optimization_barrier((bias, got[:, :-1]))
+    near = got[:, :-1]
     far = lax.ppermute(near, "zh", flip)
     bias = gather(bias, "x")
     other = lax.ppermute(bias, "core", flip)

time: 96.5 us -> 96.5 us (level)
  no operation moved by 1% of the time
where the time goes in v5:
time: 96.5 us; the launch traced here: 96 us
  blocking collectives  35 us (36%)
  starting transfers between devices  28.5 us (30%)
  waiting for transfers between devices  18.9 us (20%)
  Pallas kernels  10.6 us (11%)
  local copies, waits for them, and re-layouts  2.47 us (3%)
    all_to_all x1, blocking collectives, local(): lax.all_to_all(normalize(pair, ln_gain.reshape(1, width), w_bias.T, ring)...  21.8 us
    all_to_all x1, blocking collectives, local(): lax.all_to_all(update, 'y', 0, 0, tiled=True).reshape(rows, cols, width)  13.2 us
    ppermute x1, starting transfers between devices, local(): swap = lax.ppermute(bias, ('zl1', 'zh'), [(0, 2), (1, 0), (2, 3), (3, 1)])  12.4 us
    pallas_call x2, Pallas kernels, attend(): pl.pallas_call(functools.partial(attend_kernel, before is None), out_shap...  7.31 us
    ppermute x1, waiting for transfers between devices, local(): far = lax.ppermute(near, 'zh', flip)  6.68 us
    all_to_all x1, waiting for transfers between devices, gather(): lax.all_to_all(jnp.broadcast_to(block[None], (size,) + block.shape), axes...  5.29 us
    all_to_all x1, starting transfers between devices, gather(): lax.all_to_all(jnp.broadcast_to(block[None], (size,) + block.shape), axes...  4.96 us
    ppermute x1, waiting for transfers between devices, local(): swap = lax.ppermute(bias, ('zl1', 'zh'), [(0, 2), (1, 0), (2, 3), (3, 1)])  4.63 us
  transfers between devices with their start and end apart: 6, of which 4 were waited for; matrix products, arithmetic and copies ran while one was open for 0% of the time, Pallas kernels for 4%

profile of v5, /device:TPU:2, one launch (start us, length us, event | category | flops | bytes accessed | tf_op | source)
XLA Modules:
  0.0 96.0 jit_solution(10669827112280675352)
XLA Ops:
  0.0 2.7 %normalize.1 = bf16[8,4,48,128]{3,2,1,0:T(8,128)(2,1)} custom-call(bf16[24,48,128]{2,1,0:T(8,128)(2,1)} %pair_ref.1, f32[1,128]{1,0:T(1,128)} %bitcast.36, bf16[4,128]{1,0:T(4,128)(2,1)} %bitcast.35), custom_call_target="tpu_custom_call" | custom-call | tf_op jit(solution)/shard_map/normalize/pallas_call | solution.py:46
  2.7 21.8 %all_to_all.15 = bf16[8,4,48,128]{3,2,1,0:T(8,128)(2,1)S(1)} all-to-all(bf16[8,4,48,128]{3,2,1,0:T(8,128)(2,1)} %normalize.1), channel_id=1, replica_groups=mesh['zl1'=2,'zl0'=2,'x'=4,'core'=2,'zh'=2,'y'=8] {'y'}, dimensions={0} | all-to-all | bytes 786432 | tf_op jit(solution)/shard_map/all_to_all | solution.py:181
  24.5 0.1 pad_maximum_fusion.2
  24.6 4.3 %collective-permute-start = (bf16[96,384]{1,0:T(8,128)(2,1)S(1)}, bf16[96,384]{1,0:T(8,128)(2,1)S(1)}, u32[]{:S(2)}, u32[]{:S(2)}) collective-permute-start(bf16[96,384]{1,0:T(8,128)(2,1)S(1)} %pad_maximum_fusion.2), channel_id=1, source_target_pairs={{0,128},{128,0},{1,129},{129,1},{2,130},{130,2},{3,131},{131,3},{4... | collective-permute-start | bytes 221192 | tf_op jit(solution)/shard_map/ppermute | solution.py:186
  28.9 2.3 %collective-permute-done = bf16[96,384]{1,0:T(8,128)(2,1)S(1)} collective-permute-done((bf16[96,384]{1,0:T(8,128)(2,1)S(1)}, bf16[96,384]{1,0:T(8,128)(2,1)S(1)}, u32[]{:S(2)}, u32[]{:S(2)}) %collective-permute-start) | collective-permute-done | bytes 73760 | tf_op jit(solution)/shard_map/ppermute | solution.py:186
  31.2 0.1 select_bitcast_fusion.3
  31.3 0.7 collective-permute-start.1
  32.0 12.4 %collective-permute-start.2 = (bf16[2,96,384]{2,1,0:T(8,128)(2,1)S(1)}, bf16[2,96,384]{2,1,0:T(8,128)(2,1)S(1)}, u32[]{:S(2)}, u32[]{:S(2)}) collective-permute-start(bf16[2,96,384]{2,1,0:T(8,128)(2,1)S(1)} %pad_maximum_fusion.1), channel_id=1, source_target_pairs={{0,256},{8,0},{256,264},{264,8},{1,257},{9,1},{257,265},{265,9},{2... | collective-permute-start | bytes 442376 | tf_op jit(solution)/shard_map/ppermute | solution.py:189
  44.4 0.0 collective-permute-done.1
  44.4 4.6 %collective-permute-done.2 = bf16[2,96,384]{2,1,0:T(8,128)(2,1)S(1)} collective-permute-done((bf16[2,96,384]{2,1,0:T(8,128)(2,1)S(1)}, bf16[2,96,384]{2,1,0:T(8,128)(2,1)S(1)}, u32[]{:S(2)}, u32[]{:S(2)}) %collective-permute-start.2) | collective-permute-done | bytes 147488 | tf_op jit(solution)/shard_map/ppermute | solution.py:189
  49.1 1.2 %broadcast_in_dim.14 = bf16[4,2,2,96,384]{4,3,2,1,0:T(8,128)(2,1)} broadcast(bf16[2,2,96,384]{3,2,1,0:T(8,128)(2,1)S(1)} %pad_maximum_fusion), dimensions={1,2,3,4} | broadcast | bytes 1474560 | tf_op jit(solution)/shard_map/broadcast_in_dim | solution.py:172
  50.3 0.0 copy-start.2
  50.3 5.0 %all-to-all-start.1 = ((bf16[4,2,2,96,384]{4,3,2,1,0:T(8,128)(2,1)}), bf16[4,2,2,96,384]{4,3,2,1,0:T(8,128)(2,1)S(1)}, u32[]{:S(2)}, u32[]{:S(2)}) async-start(bf16[4,2,2,96,384]{4,3,2,1,0:T(8,128)(2,1)} %broadcast_in_dim.14), calls=%async_computation.1 | async-start | bytes 2359296 | tf_op jit(solution)/shard_map/all_to_all | solution.py:172
  55.3 4.3 %collective-permute-start.4 = (bf16[8,3,48,128]{3,2,1,0:T(8,128)(2,1)S(1)}, bf16[8,3,48,128]{3,2,1,0:T(8,128)(2,1)S(1)}, u32[]{:S(2)}, u32[]{:S(2)}) collective-permute-start(bf16[8,3,48,128]{3,2,1,0:T(8,128)(2,1)S(1)} %slice.29.own_ref), channel_id=1, source_target_pairs={{0,8},{8,0},{1,9},{9,1},{2,10},{10,2},{3,11},{11,3},{4,12},{12,4},... | collective-permute-start | bytes 884744 | tf_op jit(solution)/shard_map/ppermute | solution.py:192
  59.6 0.0 copy-done.5
  59.6 0.0 copy-done.4
  59.6 0.1 copy.13
  59.8 0.1 rev.3
  59.9 0.2 copy.17
  60.1 5.3 %all-to-all-done.1.bias_ref = bf16[4,2,2,96,384]{4,3,2,1,0:T(8,128)(2,1)S(1)} async-done(((bf16[4,2,2,96,384]{4,3,2,1,0:T(8,128)(2,1)}), bf16[4,2,2,96,384]{4,3,2,1,0:T(8,128)(2,1)S(1)}, u32[]{:S(2)}, u32[]{:S(2)}) %all-to-all-start.1) | async-done | bytes 1179680 | tf_op jit(solution)/shard_map/all_to_all | solution.py:172
  65.4 1.9 %collective-permute-start.3 = (bf16[4,2,2,96,384]{4,3,2,1,0:T(8,128)(2,1)S(1)}, bf16[4,2,2,96,384]{4,3,2,1,0:T(8,128)(2,1)S(1)}, u32[]{:S(2)}, u32[]{:S(2)}) collective-permute-start(bf16[4,2,2,96,384]{4,3,2,1,0:T(8,128)(2,1)S(1)} %all-to-all-done.1.bias_ref), channel_id=1, source_target_pairs={{0,16},{16,0},{1,17},{17,1},{2,18},{18,2},{3,19},{19,3},{4,20},{20... | collective-permute-start | bytes 3538952 | tf_op jit(solution)/shard_map/ppermute | solution.py:194
  67.3 6.7 %collective-permute-done.4.far_ref = bf16[8,3,48,128]{3,2,1,0:T(8,128)(2,1)S(1)} collective-permute-done((bf16[8,3,48,128]{3,2,1,0:T(8,128)(2,1)S(1)}, bf16[8,3,48,128]{3,2,1,0:T(8,128)(2,1)S(1)}, u32[]{:S(2)}, u32[]{:S(2)}) %collective-permute-start.4) | collective-permute-done | bytes 294944 | tf_op jit(solution)/shard_map/ppermute | solution.py:192
  74.0 0.0 copy-done
  74.0 0.0 copy-done.1
  74.0 0.0 copy-start.3
  74.0 0.6 project.1
  74.6 0.1 copy-done.3
  74.8 3.6 %attend.2.refs_0_ = f32[8,3,24,128]{3,2,1,0:T(8,128)S(1)} custom-call(s32[1]{0:T(128)} %bitcast.half_ref, bf16[4,2,2,96,384]{4,3,2,1,0:T(8,128)(2,1)S(1)} %all-to-all-done.1.bias_ref, f32[768,1]{1,0:T(8,128)S(1)} %bitcast.29, bf16[3,768,128]{2,1,0:T(8,128)(2,1)S(1)} %get-tuple-element.9.key_ref, bf16[3,128,768]{2,1,0:T(8,128)(2,1)S(1)} %get-tuple-element.10.value_ref, ...), custom_call_target="tpu_custom_call" | custom-call | flops 2000000000 | bytes 20000000 | tf_op jit(solution)/shard_map/attend/pallas_call | solution.py:158
  78.4 0.0 collective-permute-done.3.bias_ref
  78.4 3.7 %attend.3 = bf16[8,3,48,128]{3,2,1,0:T(8,128)(2,1)S(1)} custom-call(s32[1]{0:T(128)S(6)} %sub.3.half_ref, bf16[4,2,2,96,384]{4,3,2,1,0:T(8,128)(2,1)S(1)} %collective-permute-done.3.bias_ref, f32[768,1]{1,0:T(8,128)S(1)} %bitcast.30, bf16[3,768,128]{2,1,0:T(8,128)(2,1)S(1)} %get-tuple-element.9.key_ref, ...), custom_call_target="tpu_custom_call" | custom-call | flops 2000000000 | bytes 20000000 | tf_op jit(solution)/shard_map/attend/pallas_call | solution.py:158
  82.1 13.2 %all_to_all.16 = bf16[8,3,48,128]{3,2,1,0:T(8,128)(2,1)S(1)} all-to-all(bf16[8,3,48,128]{3,2,1,0:T(8,128)(2,1)S(1)} %attend.3), channel_id=1, replica_groups=mesh['zl1'=2,'zl0'=2,'x'=4,'core'=2,'zh'=2,'y'=8] {'y'}, dimensions={0} | all-to-all | bytes 589824 | tf_op jit(solution)/shard_map/all_to_all | solution.py:200
  95.3 0.7 copy.19
  (15 shorter events, 0.2 us)
Async XLA Ops:
  24.6 6.6 %collective-permute-start = (bf16[96,384]{1,0:T(8,128)(2,1)S(1)}, bf16[96,384]{1,0:T(8,128)(2,1)S(1)}, u32[]{:S(2)}, u32[]{:S(2)}) collective-permute-start(bf16[96,384]{1,0:T(8,128)(2,1)S(1)} %pad_maximum_fusion.2), channel_id=1, source_target_pairs={{0,128},{128,0},{1,129},{129,1},{2,130},{130,2},{3,131},{131,3},{4... | collective-permute-start | bytes 221192 | tf_op jit(solution)/shard_map/ppermute | solution.py:186
  31.3 13.1 %collective-permute-start.1 = (bf16[2,96,384]{2,1,0:T(8,128)(2,1)S(1)}, bf16[2,96,384]{2,1,0:T(8,128)(2,1)S(1)}, u32[]{:S(2)}, u32[]{:S(2)}) collective-permute-start(bf16[2,96,384]{2,1,0:T(8,128)(2,1)S(1)} %pad_maximum_fusion.1), channel_id=1, source_target_pairs={{0,0},{8,256},{256,8},{264,264},{1,1},{9,257},{257,9},{265,265},{2... | collective-permute-start | bytes 442376 | tf_op jit(solution)/shard_map/ppermute | solution.py:188
  32.0 17.0 %collective-permute-start.2 = (bf16[2,96,384]{2,1,0:T(8,128)(2,1)S(1)}, bf16[2,96,384]{2,1,0:T(8,128)(2,1)S(1)}, u32[]{:S(2)}, u32[]{:S(2)}) collective-permute-start(bf16[2,96,384]{2,1,0:T(8,128)(2,1)S(1)} %pad_maximum_fusion.1), channel_id=1, source_target_pairs={{0,256},{8,0},{256,264},{264,8},{1,257},{9,1},{257,265},{265,9},{2... | collective-permute-start | bytes 442376 | tf_op jit(solution)/shard_map/ppermute | solution.py:189
  50.3 9.3 %copy-start.5 = (s32[768]{0:T(1024)S(1)}, s32[768]{0:T(1024)}, u32[]{:S(2)}) copy-start(s32[768]{0:T(1024)} %param.10) | copy-start | bytes 9220
  50.3 9.4 %copy-start.4 = (bf16[128,128]{1,0:T(8,128)(2,1)S(1)}, bf16[128,128]{1,0:T(8,128)(2,1)}, u32[]{:S(2)}) copy-start(bf16[128,128]{1,0:T(8,128)(2,1)} %param.14) | copy-start | bytes 98308
  50.3 23.7 %copy-start = (bf16[128,128]{1,0:T(8,128)(2,1)S(1)}, bf16[128,128]{1,0:T(8,128)(2,1)}, u32[]{:S(2)}) copy-start(bf16[128,128]{1,0:T(8,128)(2,1)} %wq_ref.1) | copy-start | bytes 98308
  50.3 23.7 %copy-start.1 = (bf16[128,128]{1,0:T(8,128)(2,1)S(1)}, bf16[128,128]{1,0:T(8,128)(2,1)}, u32[]{:S(2)}) copy-start(bf16[128,128]{1,0:T(8,128)(2,1)} %wk_ref.1) | copy-start | bytes 98308
  50.3 23.7 %copy-start.2 = (bf16[128,128]{1,0:T(8,128)(2,1)S(1)}, bf16[128,128]{1,0:T(8,128)(2,1)}, u32[]{:S(2)}) copy-start(bf16[128,128]{1,0:T(8,128)(2,1)} %wg_ref.1) | copy-start | bytes 98308
  50.3 15.1 %all-to-all-start.1 = ((bf16[4,2,2,96,384]{4,3,2,1,0:T(8,128)(2,1)}), bf16[4,2,2,96,384]{4,3,2,1,0:T(8,128)(2,1)S(1)}, u32[]{:S(2)}, u32[]{:S(2)}) async-start(bf16[4,2,2,96,384]{4,3,2,1,0:T(8,128)(2,1)} %broadcast_in_dim.14), calls=%async_computation.1 | async-start | bytes 2359296 | tf_op jit(solution)/shard_map/all_to_all | solution.py:172
  55.3 18.7 %collective-permute-start.4 = (bf16[8,3,48,128]{3,2,1,0:T(8,128)(2,1)S(1)}, bf16[8,3,48,128]{3,2,1,0:T(8,128)(2,1)S(1)}, u32[]{:S(2)}, u32[]{:S(2)}) collective-permute-start(bf16[8,3,48,128]{3,2,1,0:T(8,128)(2,1)S(1)} %slice.29.own_ref), channel_id=1, source_target_pairs={{0,8},{8,0},{1,9},{9,1},{2,10},{10,2},{3,11},{11,3},{4,12},{12,4},... | collective-permute-start | bytes 884744 | tf_op jit(solution)/shard_map/ppermute | solution.py:192
  65.4 13.0 %collective-permute-start.3 = (bf16[4,2,2,96,384]{4,3,2,1,0:T(8,128)(2,1)S(1)}, bf16[4,2,2,96,384]{4,3,2,1,0:T(8,128)(2,1)S(1)}, u32[]{:S(2)}, u32[]{:S(2)}) collective-permute-start(bf16[4,2,2,96,384]{4,3,2,1,0:T(8,128)(2,1)S(1)} %all-to-all-done.1.bias_ref), channel_id=1, source_target_pairs={{0,16},{16,0},{1,17},{17,1},{2,18},{18,2},{3,19},{19,3},{4,20},{20... | collective-permute-start | bytes 3538952 | tf_op jit(solution)/shard_map/ppermute | solution.py:194
  74.0 0.8 copy-start.3
